TPU v7x, 512 devices: a whole 4x8x8 slice. The times are simulated.
512 devices in a mesh: src: 32 (over y, z_hi), rcv: 16 (over z_lo, x, core).
Axes of the slice: x: 4, y: 8, z: 8 (z_hi: 4, z_lo: 2; z = z_hi * 2 + z_lo), core: 2. Of those that a mesh axis runs over, the one named last changes fastest.
Arguments:
- traces: bfloat16 [32, 16, 256, 2048], P('src', 'rcv'), may hold values from -6 to 6
- source_ids: int32 [32, 16, 256], P('src', 'rcv'), may hold values from 0 to 31
- receiver_ids: int32 [32, 16, 256], P('src', 'rcv'), may hold values from 0 to 31
- offset_ids: int32 [32, 16, 256], P('src', 'rcv'), may hold values from 0 to 63
- receiver_init: float32 [512, 1024], P('rcv'), may hold values from -6 to 6
- offset_init: float32 [64, 1024], replicated, may hold values from -6 to 6
Outputs:
- source_terms: float32 [1024, 1024], P('src')
- receiver_terms: float32 [512, 1024], P('rcv')
- offset_terms: float32 [64, 1024], replicated
- residual: float32 [32, 16, 256, 1024], P('src', 'rcv')
All inputs are finite; a program needn't handle non-finite values.
Results may differ from a plain program's by a relative error of at most 0.0034.
Values sent between devices are 32-bit elements; how exact they have to be, the bound alone decides.
A program may use at most 64 MiB of HBM per device.

v0:
```python
import jax
import jax.numpy as jnp
from jax import lax
from jax.sharding import PartitionSpec as P

NSRC_DEV = 32


def dft_tables(samples, start, count):
    times = jnp.arange(samples, dtype=jnp.int32)[:, None]
    bins = (start + jnp.arange(count, dtype=jnp.int32))[None, :]
    phase = times * bins % samples
    angle = phase.astype(jnp.float32) * (2.0 * 3.141592653589793 / samples)
    return jnp.concatenate([jnp.cos(angle), -jnp.sin(angle)], axis=1).astype(jnp.bfloat16)


def log_spectra(block, bins):
    samples = block.shape[1]
    width = min(256, bins)
    pieces = []
    for first in range(0, bins, width):
        tables = dft_tables(samples, first, width)
        both = jnp.dot(block, tables, preferred_element_type=jnp.float32)
        real = both[:, :width]
        imag = both[:, width:]
        power = (real * real + imag * imag) / samples
        pieces.append(0.5 * jnp.log(power + 0.25))
    return jnp.concatenate(pieces, axis=1)


def one_hot(labels, count):
    return (labels[None, :] == jnp.arange(count, dtype=jnp.int32)[:, None]).astype(jnp.float32)


def collect(hot, values):
    return jnp.dot(hot, values, precision=lax.Precision.HIGHEST, preferred_element_type=jnp.float32)


def spread(hot, terms):
    return jnp.dot(
        hot.T, terms, precision=lax.Precision.HIGHEST, preferred_element_type=jnp.float32
    )


def on_device(traces, source_ids, receiver_ids, offset_ids, receiver_init, offset_init):
    bins = receiver_init.shape[1]
    spectra = log_spectra(traces[0, 0], bins)
    src_hot = one_hot(source_ids[0, 0], NSRC_DEV)
    rcv_hot = one_hot(receiver_ids[0, 0], receiver_init.shape[0])
    off_hot = one_hot(offset_ids[0, 0], offset_init.shape[0])
    rcv_count = lax.psum(jnp.sum(rcv_hot, axis=1), "src")
    off_count = lax.psum(jnp.sum(off_hot, axis=1), ("src", "rcv"))
    off_before = spread(off_hot, offset_init)
    base = spectra - spread(rcv_hot, receiver_init) - off_before
    src_total, src_count = lax.psum((collect(src_hot, base), jnp.sum(src_hot, axis=1)), "rcv")
    source_terms = src_total / (src_count + 1.0)[:, None]
    src_along = spread(src_hot, source_terms)
    after = spectra - src_along - off_before
    rcv_total = lax.psum(collect(rcv_hot, after), "src")
    receiver_terms = rcv_total / (rcv_count + 1.0)[:, None]
    later = spectra - src_along - spread(rcv_hot, receiver_terms)
    off_total = lax.psum(collect(off_hot, later), ("src", "rcv"))
    offset_terms = off_total / (off_count + 1.0)[:, None]
    residual = later - spread(off_hot, offset_terms)
    return (source_terms, receiver_terms, offset_terms, residual[None, None])


def solution(mesh):
    placed = (
        P("src", "rcv", None, None),
        P("src", "rcv", None),
        P("src", "rcv", None),
        P("src", "rcv", None),
        P("rcv", None),
        P(),
    )
    return jax.shard_map(
        on_device,
        mesh=mesh,
        in_specs=placed,
        out_specs=(P("src", None), P("rcv", None), P(), P("src", "rcv", None, None)),
        check_vma=False,
    )
```

profile of v0, /device:TPU:1, one launch (start us, length us, event | category | flops | bytes accessed | tf_op | source)
XLA Modules:
  0.0 835.0 jit_solution(1532966133197743297)
XLA Ops:
  7.3 8.5 %negate_convert_fusion.3 = (bf16[2048,256]{1,0:T(8,128)(2,1)S(1)}, bf16[2048,256]{1,0:T(8,128)(2,1)S(1)}) fusion(), kind=kLoop, calls=%fused_computation.52 | loop fusion | flops 8912896 | bytes 2097152 | tf_op jit(solution)/shard_map/convert.7
  15.8 8.6 %cosine_convert_fusion.1 = (bf16[2048,256]{1,0:T(8,128)(2,1)S(1)}, bf16[2048,256]{1,0:T(8,128)(2,1)S(1)}) fusion(s32[256]{0:T(256)S(1)} %iota_add_fusion.1), kind=kLoop, calls=%fused_computation.45 | loop fusion | flops 8912896 | bytes 2098176 | tf_op jit(solution)/shard_map/convert.2
  24.5 8.6 %cosine_convert_fusion = (bf16[2048,256]{1,0:T(8,128)(2,1)S(1)}, bf16[2048,256]{1,0:T(8,128)(2,1)S(1)}) fusion(s32[256]{0:T(256)S(1)} %iota_add_fusion), kind=kLoop, calls=%fused_computation.41 | loop fusion | flops 8912896 | bytes 2098176 | tf_op jit(solution)/shard_map/convert
  33.1 8.6 %cosine_convert_fusion.2 = (bf16[2048,256]{1,0:T(8,128)(2,1)S(1)}, bf16[2048,256]{1,0:T(8,128)(2,1)S(1)}) fusion(s32[256]{0:T(256)S(1)} %iota_add_fusion.2), kind=kLoop, calls=%fused_computation.49 | loop fusion | flops 8912896 | bytes 2098176 | tf_op jit(solution)/shard_map/convert.4
  41.7 0.8 fusion.48
  42.6 0.8 fusion.51
  43.5 0.8 fusion.45
  44.2 0.8 fusion.42
  45.2 0.7 copy-done.7
  46.6 0.6 fusion.40
  47.3 1.3 fusion.85
  49.0 33.4 %psum.43 = f32[32]{0:T(128)S(1)} all-reduce(f32[32]{0:T(128)S(1)} %convert_reduce_fusion.2), channel_id=1, replica_groups=mesh['src'=32,'rcv'=16] {'rcv'}, use_global_device_ids=true, to_apply=%region_2.3 | all-reduce | flops 32 | bytes 256 | tf_op jit(solution)/shard_map/psum | solution.py:55
  82.4 69.5 %psum.45 = f32[32]{0:T(128)S(1)} all-reduce(f32[32]{0:T(128)S(1)} %convert_reduce_fusion.1), channel_id=1, replica_groups=mesh['src'=32,'rcv'=16] {'src'}, use_global_device_ids=true, to_apply=%region_5.6 | all-reduce | flops 32 | bytes 256 | tf_op jit(solution)/shard_map/psum | solution.py:51
  151.9 109.8 %psum.47 = f32[64]{0:T(128)S(1)} all-reduce(f32[64]{0:T(128)S(1)} %convert_reduce_fusion), channel_id=1, replica_groups=mesh['src'=32,'rcv'=16] {'src','rcv'}, use_global_device_ids=true, to_apply=%region_8.9 | all-reduce | flops 64 | bytes 512 | tf_op jit(solution)/shard_map/psum | solution.py:52
  261.7 1.0 broadcast_divide_fusion.2
  262.7 1.8 convolution_subtract_fusion.1
  264.5 1.3 fusion.58
  265.9 271.9 %all-reduce.6.cloned.1.call-done = f32[32,1024]{1,0:T(8,128)} async-done(((f32[32,1024]{1,0:T(8,128)}), f32[32,1024]{1,0:T(8,128)}) %all-reduce.6.cloned.1.call-update) | async-done | bytes 131088 | tf_op jit(solution)/shard_map/psum | solution.py:59
  537.8 1.0 broadcast_divide_fusion.1
  538.8 0.6 convolution_subtract_fusion
  539.5 1.4 fusion.80
  540.9 284.6 %all-reduce.8.cloned.1.call-done = f32[64,1024]{1,0:T(8,128)} async-done(((f32[64,1024]{1,0:T(8,128)}), f32[64,1024]{1,0:T(8,128)}) %all-reduce.8.cloned.1.call-update) | async-done | bytes 262160 | tf_op jit(solution)/shard_map/psum | solution.py:62
  825.4 1.0 broadcast_divide_fusion
  827.2 1.3 copy.21
  (44 shorter events, 2.2 us)
Async XLA Ops:
  7.2 34.6 %copy-start = (bf16[1,1,256,2048]{3,2,1,0:T(8,128)(2,1)S(1)}, bf16[1,1,256,2048]{3,2,1,0:T(8,128)(2,1)}, u32[]{:S(2)}) copy-start(bf16[1,1,256,2048]{3,2,1,0:T(8,128)(2,1)} %param.6) | copy-start | bytes 3145732
  7.2 254.5 %all-reduce.4.cloned.1.call-start = ((), (), s32[]{:S(2)}) async-start(), calls=%async_computation | async-start | bytes 262144 | tf_op jit(solution)/shard_map/psum | solution.py:55
  43.5 3.1 copy-start.1
  45.0 1.0 copy-start.7
  45.0 0.9 copy-start.10
  45.2 2.1 copy-start.2
  45.2 2.1 copy-start.3
  45.2 1.4 copy-start.8
  45.2 1.4 copy-start.9
  46.6 0.7 copy-start.11
  48.6 489.2 %all-reduce.6.cloned.1.call-start = ((), (), s32[]{:S(2)}) async-start(), calls=%async_computation.1 | async-start | bytes 262144 | tf_op jit(solution)/shard_map/psum | solution.py:59
  262.7 1.8 copy-start.5
  265.8 559.6 %all-reduce.8.cloned.1.call-start = ((), (), s32[]{:S(2)}) async-start(), calls=%async_computation.2 | async-start | bytes 524288 | tf_op jit(solution)/shard_map/psum | solution.py:62
  538.8 0.7 copy-start.6
  826.5 0.7 copy-start.4
Sparse Core Ops, SparseCore 0:
  48.7 131.9 all-reduce.3
  266.0 271.7 all-reduce.5
  543.4 282.0 all-reduce.7
where the time goes:
time: 835 us
  waiting for transfers between devices  557 us (67%)
  blocking collectives  213 us (26%)
  other arithmetic  38.1 us (5%)
  between operations  14.1 us (2%)
  matrix products  11.3 us (1%)
    psum x1, waiting for transfers between devices, on_device(): off_total = lax.psum(collect(off_hot, later), ('src', 'rcv'))  285 us
    psum x1, waiting for transfers between devices, on_device(): rcv_total = lax.psum(collect(rcv_hot, after), 'src')  272 us
    psum x1, blocking collectives, on_device(): off_count = lax.psum(jnp.sum(off_hot, axis=1), ('src', 'rcv'))  110 us
    psum x1, blocking collectives, on_device(): rcv_count = lax.psum(jnp.sum(rcv_hot, axis=1), 'src')  69.5 us
    another operation x4, other arithmetic  34.4 us
    psum x1, blocking collectives, on_device(): lax.psum((collect(src_hot, base), jnp.sum(src_hot, axis=1)), 'rcv')  33.4 us
  transfers between devices with their start and end apart: 3, of which 2 were waited for; matrix products, arithmetic and copies ran while one was open for 0% of the time, Pallas kernels for 0%

commit v1 on v0

v1 whole, which is shorter than its diff:
```python
import functools

import jax
import jax.numpy as jnp
import ml_dtypes
import numpy as np
from jax import lax
from jax.experimental import pallas as pl
from jax.experimental.pallas import tpu as pltpu
from jax.sharding import PartitionSpec as P

NSRC = 32
NRCV = 32
NOFF = 64
ROWS = NSRC + NRCV + NOFF
MESH = pl.DeviceIdType.MESH
HIGHEST = lax.Precision.HIGHEST


def dft_tables(samples, bins, chunks):
    times = np.arange(samples, dtype=np.int64)[:, None]
    freqs = np.arange(bins, dtype=np.int64)[None, :]
    phase = (times * freqs) % samples
    angle = phase.astype(np.float32) * np.float32(2.0 * 3.141592653589793 / samples)
    cosine = np.cos(angle).astype(ml_dtypes.bfloat16)
    sine = (-np.sin(angle)).astype(ml_dtypes.bfloat16)
    width = bins // chunks
    return np.stack(
        [
            np.concatenate([t[:, c * width : (c + 1) * width] for t in (cosine, sine)], axis=1)
            for c in range(chunks)
        ]
    )


def hot_rows(src, rcv, off):
    parts = []
    for ids, count in ((src, NSRC), (rcv, NRCV), (off, NOFF)):
        rows = lax.broadcasted_iota(jnp.int32, (count, ids.shape[1]), 0)
        parts.append((rows == ids).astype(jnp.float32))
    return jnp.concatenate(parts, axis=0)


def split(values):
    high = values.astype(jnp.bfloat16)
    low = (values - high.astype(jnp.float32)).astype(jnp.bfloat16)
    return high, low


def dot(a, b):
    return jnp.dot(a, b, preferred_element_type=jnp.float32)


def local_kernel(
    samples, traces_ref, tables_ref, src_ref, rcv_ref, off_ref, rinit_ref, oinit_ref,
    spectra_ref, sums_ref, gram_ref,
):
    width = spectra_ref.shape[1]
    both = dot(traces_ref[...], tables_ref[0])
    real, imag = both[:, :width], both[:, width:]
    spectra = 0.5 * jnp.log((real * real + imag * imag) * (1.0 / samples) + 0.25)
    spectra_ref[...] = spectra

    hot = hot_rows(src_ref[...], rcv_ref[...], off_ref[...]).astype(jnp.bfloat16)
    gram = lax.dot_general(hot, hot, (((1,), (1,)), ((), ())), preferred_element_type=jnp.float32)
    gram_ref[...] = gram
    row = lax.broadcasted_iota(jnp.int32, (ROWS, ROWS), 0)
    lane = lax.broadcasted_iota(jnp.int32, (ROWS, ROWS), 1)
    from_rcv = (lane >= NSRC) & (lane < NSRC + NRCV) & (row < NSRC)
    from_off = (lane >= NSRC + NRCV) & (row < NSRC + NRCV)
    before = jnp.where(from_rcv | from_off, gram, 0.0).astype(jnp.bfloat16)
    zeros = jnp.zeros((NSRC, width), jnp.float32)
    init = jnp.concatenate([zeros, rinit_ref[...], oinit_ref[...]], axis=0)
    spec_high, spec_low = split(spectra)
    init_high, init_low = split(init)
    sums = (dot(hot, spec_high) - dot(before, init_high)) + (dot(hot, spec_low) - dot(before, init_low))
    turned = sums.T
    slices, rows, _ = sums_ref.shape
    per = rows - NSRC
    for k in range(slices):
        sums_ref[k, :per, :] = turned[k * per : (k + 1) * per]
        sums_ref[k, per:, :] = gram[:NSRC]


def spectra_and_sums(traces, src, rcv, off, receiver_init, offset_init, parts):
    traces_n, samples = traces.shape
    bins = receiver_init.shape[1]
    chunks = max(1, bins // 256)
    width = bins // chunks
    per = bins // parts
    tables = jnp.asarray(dft_tables(samples, bins, chunks))
    whole = lambda c: (0, 0)
    along = lambda c: (0, c)
    return pl.pallas_call(
        functools.partial(local_kernel, samples),
        grid=(chunks,),
        in_specs=[
            pl.BlockSpec((traces_n, samples), whole),
            pl.BlockSpec((1, samples, 2 * width), lambda c: (c, 0, 0)),
            pl.BlockSpec((1, traces_n), whole),
            pl.BlockSpec((1, traces_n), whole),
            pl.BlockSpec((1, traces_n), whole),
            pl.BlockSpec((NRCV, width), along),
            pl.BlockSpec((NOFF, width), along),
        ],
        out_specs=[
            pl.BlockSpec((traces_n, width), along),
            pl.BlockSpec((parts // chunks, per + NSRC, ROWS), lambda c: (c, 0, 0)),
            pl.BlockSpec((ROWS, ROWS), whole),
        ],
        out_shape=[
            jax.ShapeDtypeStruct((traces_n, bins), jnp.float32),
            jax.ShapeDtypeStruct((parts, per + NSRC, ROWS), jnp.float32),
            jax.ShapeDtypeStruct((ROWS, ROWS), jnp.float32),
        ],
        compiler_params=pltpu.CompilerParams(
            dimension_semantics=("arbitrary",), vmem_limit_bytes=32 * 1024 * 1024
        ),
    )(traces, tables, src, rcv, off, receiver_init, offset_init)


def pick(tiles, lane):
    out = pltpu.roll(tiles[0], ROWS - 32, 1)
    out = jnp.where(lane < 32, out, tiles[1])
    out = jnp.where(lane < 64, out, pltpu.roll(tiles[2], 32, 1))
    return jnp.where(lane < 96, out, pltpu.roll(tiles[3], 64, 1))


def sweep_kernel(
    nj, ny, nz, sums_ref, gram_ref, terms_ref,
    a_buf, gy_buf, gz_buf, gr_buf, p_buf, b1_buf, b2_buf, c_buf, d_out, d_buf,
    a_send, a_recv, gy_send, gy_recv, gz_send, gz_recv, gr_send, gr_recv,
    b1_send, b1_recv, b2_send, b2_recv, c_send, c_recv, d_send, d_recv,
):
    i = lax.axis_index("src")
    j = lax.axis_index("rcv")
    y = i // nz
    z = i % nz
    per = a_buf.shape[1] - NSRC
    tiles = nj * NRCV // ROWS

    def over_j(d):
        peer = (j + d) % nj
        return peer, (i, peer)

    def over_y(d):
        peer = (y + d) % ny
        return peer, (peer * nz + z, j)

    def over_z(d):
        peer = (z + d) % nz
        return peer, (y * nz + peer, j)

    def loop(n, body):
        def step(d, carry):
            body(d)
            return carry

        lax.fori_loop(1, n, step, 0)

    def send(n, over, me, source, buf, send_sem, recv_sem):
        def body(d):
            peer, device = over(d)
            pltpu.make_async_remote_copy(
                src_ref=source(peer), dst_ref=buf.at[me], send_sem=send_sem.at[d],
                recv_sem=recv_sem.at[me], device_id=device, device_id_type=MESH,
            ).start()

        loop(n, body)

    def arrive(n, over, buf, send_sem, recv_sem):
        def body(d):
            peer, device = over(d)
            pltpu.make_async_remote_copy(
                src_ref=buf.at[peer], dst_ref=buf.at[peer], send_sem=send_sem.at[d],
                recv_sem=recv_sem.at[peer], device_id=device, device_id_type=MESH,
            ).wait_recv()

        loop(n, body)

    def sent(n, over, me, source, buf, send_sem, recv_sem):
        def body(d):
            peer, device = over(d)
            pltpu.make_async_remote_copy(
                src_ref=source(peer), dst_ref=buf.at[me], send_sem=send_sem.at[d],
                recv_sem=recv_sem.at[me], device_id=device, device_id_type=MESH,
            ).wait_send()

        loop(n, body)

    barrier = pltpu.get_barrier_semaphore()
    for n, over in ((nj, over_j), (ny, over_y), (nz, over_z)):
        def greet(d, over=over):
            pl.semaphore_signal(barrier, inc=1, device_id=over(d)[1], device_id_type=MESH)

        loop(n, greet)
    pl.semaphore_wait(barrier, nj + ny + nz - 3)

    count_y = (ny, over_y, y, lambda p: gy_buf.at[y], gy_buf, gy_send, gy_recv)
    gy_buf[y] = gram_ref[NSRC : NSRC + NRCV, :]
    send(*count_y)
    sums_j = (nj, over_j, j, lambda p: sums_ref.at[p], a_buf, a_send, a_recv)
    send(*sums_j)
    a_buf[j] = sums_ref[j]

    count_z = (nz, over_z, z, lambda p: gz_buf.at[z], gz_buf, gz_send, gz_recv)
    arrive(ny, over_y, gy_buf, gy_send, gy_recv)
    gz_buf[z] = jnp.sum(gy_buf[...], axis=0)
    send(*count_z)

    arrive(nj, over_j, a_buf, a_send, a_recv)
    total = jnp.sum(a_buf[...], axis=0)
    lane = lax.broadcasted_iota(jnp.int32, (per, ROWS), 1)
    n_src = jnp.sum(total[per:], axis=0, keepdims=True)
    src_terms = jnp.where(lane < NSRC, total[:per] / (n_src + 1.0), 0.0)
    counts = jnp.concatenate([a_buf[q, per:, :] for q in range(nj)], axis=1)
    along = jnp.dot(
        src_terms[:, :NSRC], counts, precision=HIGHEST, preferred_element_type=jnp.float32
    )
    left = [a_buf[q, :per, :] - along[:, q * ROWS : (q + 1) * ROWS] for q in range(nj)]
    packed = [pick(left[4 * t : 4 * t + 4], lane) for t in range(tiles)]
    packed.append(functools.reduce(lambda a, b: a + b, left))
    few = per // ny
    for t in range(tiles + 1):
        p_buf[:, :, t * ROWS : (t + 1) * ROWS] = packed[t].reshape(ny, few, ROWS)
    part_y = (ny, over_y, y, lambda p: p_buf.at[p], b1_buf, b1_send, b1_recv)
    send(*part_y)
    b1_buf[y] = p_buf[y]

    count_j = (nj, over_j, j, lambda p: gr_buf.at[j], gr_buf, gr_send, gr_recv)
    arrive(nz, over_z, gz_buf, gz_send, gz_recv)
    gr_buf[j] = jnp.sum(gz_buf[...], axis=0)
    send(*count_j)

    part_z = (nz, over_z, z, lambda p: b2_buf.at[z], b2_buf, b2_send, b2_recv)
    arrive(ny, over_y, b1_buf, b1_send, b1_recv)
    b2_buf[z] = jnp.sum(b1_buf[...], axis=0)
    send(*part_z)

    arrive(nj, over_j, gr_buf, gr_send, gr_recv)
    by_rcv = gr_buf[...]
    columns = [jnp.sum(by_rcv[q], axis=0, keepdims=True) for q in range(nj)]
    n_off = functools.reduce(lambda a, b: a + b, columns)
    n_rcv = [
        pick([jnp.broadcast_to(c, (few, ROWS)) for c in columns[4 * t : 4 * t + 4]], lane[:few])
        for t in range(tiles)
    ]
    n_rcv = jnp.concatenate(n_rcv, axis=1)
    arrive(nz, over_z, b2_buf, b2_send, b2_recv)
    reduced = b2_buf[0]
    for q in range(1, nz):
        reduced = reduced + b2_buf[q]
    rcv_terms = reduced[:, : tiles * ROWS] / (n_rcv + 1.0)
    later = reduced[:, tiles * ROWS :] - jnp.dot(
        rcv_terms, by_rcv.reshape(nj * NRCV, ROWS), precision=HIGHEST,
        preferred_element_type=jnp.float32,
    )
    off_terms = later / (n_off + 1.0)
    c_buf[y] = jnp.concatenate([rcv_terms, off_terms], axis=1)
    terms_y = (ny, over_y, y, lambda p: c_buf.at[y], c_buf, c_send, c_recv)
    send(*terms_y)
    arrive(ny, over_y, c_buf, c_send, c_recv)

    off_tile = c_buf[:, :, tiles * ROWS :].reshape(per, ROWS)
    for t in range(tiles):
        tile = c_buf[:, :, t * ROWS : (t + 1) * ROWS].reshape(per, ROWS)
        for q in range(4):
            turned = tile if q == 1 else pltpu.roll(tile, (32 - 32 * q) % ROWS, 1)
            d_out[4 * t + q] = jnp.where(
                lane < NSRC, src_terms, jnp.where(lane < NSRC + NRCV, turned, off_tile)
            )
    back_j = (nj, over_j, j, lambda p: d_out.at[p], d_buf, d_send, d_recv)
    send(*back_j)
    d_buf[j] = d_out[j]
    arrive(nj, over_j, d_buf, d_send, d_recv)
    terms_ref[...] = d_buf[...].reshape(nj * per, ROWS).T

    for copies in (count_y, sums_j, count_z, part_y, count_j, part_z, terms_y, back_j):
        sent(*copies)


def sweep(sums, gram, nj, ny, nz):
    per = sums.shape[1] - NSRC
    bins = nj * per
    few = per // ny
    wide = nj * NRCV + ROWS
    vmem = pl.BlockSpec(memory_space=pltpu.VMEM)
    f32 = jnp.float32
    dma = lambda n: [pltpu.SemaphoreType.DMA((n,)), pltpu.SemaphoreType.DMA((n,))]
    return pl.pallas_call(
        functools.partial(sweep_kernel, nj, ny, nz),
        in_specs=[vmem, vmem],
        out_specs=vmem,
        out_shape=jax.ShapeDtypeStruct((ROWS, bins), f32),
        scratch_shapes=[
            pltpu.VMEM((nj, per + NSRC, ROWS), f32),
            pltpu.VMEM((ny, NRCV, ROWS), f32),
            pltpu.VMEM((nz, NRCV, ROWS), f32),
            pltpu.VMEM((nj, NRCV, ROWS), f32),
            pltpu.VMEM((ny, few, wide), f32),
            pltpu.VMEM((ny, few, wide), f32),
            pltpu.VMEM((nz, few, wide), f32),
            pltpu.VMEM((ny, few, wide), f32),
            pltpu.VMEM((nj, per, ROWS), f32),
            pltpu.VMEM((nj, per, ROWS), f32),
            *dma(nj), *dma(ny), *dma(nz), *dma(nj), *dma(ny), *dma(nz), *dma(ny), *dma(nj),
        ],
        compiler_params=pltpu.CompilerParams(
            collective_id=0, has_side_effects=True, vmem_limit_bytes=32 * 1024 * 1024
        ),
    )(sums, gram)


def on_device(
    nj, ny, nz, traces, source_ids, receiver_ids, offset_ids, receiver_init, offset_init
):
    src, rcv, off = source_ids[0], receiver_ids[0], offset_ids[0]
    spectra, sums, gram = spectra_and_sums(
        traces[0, 0], src, rcv, off, receiver_init, offset_init, nj
    )
    terms = sweep(sums, gram, nj, ny, nz)
    hot = hot_rows(src, rcv, off)
    residual = spectra - jnp.dot(
        hot.T, terms, precision=HIGHEST, preferred_element_type=jnp.float32
    )
    return (
        terms[:NSRC], terms[NSRC : NSRC + NRCV], terms[NSRC + NRCV :], residual[None, None]
    )


def solution(mesh):
    nsrc, nj = mesh.shape["src"], mesh.shape["rcv"]
    nz = 4 if nsrc >= 32 else 2
    ny = nsrc // nz
    placed = (
        P("src", "rcv", None, None),
        P("src", "rcv", None),
        P("src", "rcv", None),
        P("src", "rcv", None),
        P("rcv", None),
        P(),
    )
    return jax.shard_map(
        functools.partial(on_device, nj, ny, nz),
        mesh=mesh,
        in_specs=placed,
        out_specs=(P("src", None), P("rcv", None), P(), P("src", "rcv", None, None)),
        check_vma=False,
    )
```

time: 835 us -> 71.7 us (0.09)
  waiting for transfers between devices: 557 us -> 0 us
  blocking collectives: 213 us -> 0 us
  Pallas kernels: 0 us -> 57.3 us
  other arithmetic: 38.1 us -> 1.41 us
  between operations: 14.1 us -> 0.67 us
  matrix products: 11.3 us -> 1.63 us
    psum x3 -> x0, waiting for transfers between devices: 556 us -> none  [the longest x1 285 us: on_device(): off_total = lax.psum(collect(off_hot, later), ('src', 'rcv'))]
    psum x3 -> x0, blocking collectives: 213 us -> none  [the longest x1 110 us: on_device(): off_count = lax.psum(jnp.sum(off_hot, axis=1), ('src', 'rcv'))]
    pallas_call x0 -> x2, Pallas kernels: none -> 57.3 us  [the longest x1 53.1 us: sweep(): pl.pallas_call(functools.partial(sweep_kernel, nj, ny, nz), in_specs=[vme...]
    another operation x4 -> x0, other arithmetic: 34.4 us -> none
    dot_general x12 -> x1, matrix products: 11.3 us -> 1.63 us  [on_device(): jnp.dot(hot.T, terms, precision=HIGHEST, preferred_element_type=jnp.float32)]
  transfers between devices with their start and end apart: 3 -> 0, of which waited for: 2 -> 0; matrix products, arithmetic and copies ran while one was open for 0% -> 0% of each run, Pallas kernels for 0% -> 0%
where the time goes in v1:
time: 71.7 us; the launch traced here: 71 us
  Pallas kernels  57.3 us (80%)
  local copies, waits for them, and re-layouts  9.93 us (14%)
  matrix products  1.63 us (2%)
  other arithmetic  1.41 us (2%)
    pallas_call x1, Pallas kernels, sweep(): pl.pallas_call(functools.partial(sweep_kernel, nj, ny, nz), in_specs=[vme...  53.1 us
    unnamed x14, local copies, waits for them, and re-layouts  8.49 us
    pallas_call x1, Pallas kernels, spectra_and_sums(): pl.pallas_call(functools.partial(local_kernel, samples), grid=(chunks,),...  4.18 us
    dot_general x1, matrix products, on_device(): jnp.dot(hot.T, terms, precision=HIGHEST, preferred_element_type=jnp.float32)  1.63 us

profile of v1, /device:TPU:1, one launch (start us, length us, event | category | flops | bytes accessed | tf_op | source)
XLA Modules:
  0.0 71.0 jit_solution(6383090433440229145)
XLA Ops:
  0.6 0.7 iota_compare_fusion
  1.3 0.7 %iota_compare_fusion.1 = (pred[32,256]{1,0:T(32,128)(4,1)S(1)}, pred[32,256]{1,0:T(32,128)(4,1)S(1)}) fusion(s32[256]{0:T(256)} %bitcast.13, s32[256]{0:T(256)} %bitcast.11), kind=kLoop, calls=%fused_computation.8 | loop fusion | flops 16384 | bytes 18432 | tf_op jit(solution)/shard_map/eq | solution.py:40
  2.0 0.0 copy-start
  2.1 3.4 %copy-done = bf16[4,2048,512]{2,1,0:T(8,128)(2,1)S(1)} copy-done((bf16[4,2048,512]{2,1,0:T(8,128)(2,1)S(1)}, bf16[4,2048,512]{2,1,0:T(8,128)(2,1)}, u32[]{:S(2)}) %copy-start) | copy-done | bytes 8388632
  5.4 0.0 copy-start.1
  5.4 1.2 %copy-done.1 = bf16[1,1,256,2048]{3,2,1,0:T(8,128)(2,1)S(1)} copy-done((bf16[1,1,256,2048]{3,2,1,0:T(8,128)(2,1)S(1)}, bf16[1,1,256,2048]{3,2,1,0:T(8,128)(2,1)}, u32[]{:S(2)}) %copy-start.1) | copy-done | bytes 1048600
  6.7 0.0 copy-start.2
  6.7 0.9 %copy-done.2 = f32[64,1024]{1,0:T(8,128)S(1)} copy-done((f32[64,1024]{1,0:T(8,128)S(1)}, f32[64,1024]{1,0:T(8,128)}, u32[]{:S(2)}) %copy-start.2) | copy-done | bytes 262168
  7.6 0.0 copy-start.3
  7.6 0.9 %copy-done.3 = f32[32,1024]{1,0:T(8,128)S(1)} copy-done((f32[32,1024]{1,0:T(8,128)S(1)}, f32[32,1024]{1,0:T(8,128)}, u32[]{:S(2)}) %copy-start.3) | copy-done | bytes 131096
  8.5 0.0 copy-start.4
  8.5 0.7 copy-done.4
  9.2 0.0 copy-start.5
  9.2 0.7 copy-done.5
  9.9 0.0 copy-start.6
  9.9 0.7 copy-done.6
  10.5 4.2 %shard_map.102 = (f32[256,1024]{1,0:T(8,128)S(1)}, f32[16,96,128]{2,1,0:T(8,128)S(1)}, f32[128,128]{1,0:T(8,128)S(1)}) custom-call(bf16[256,2048]{1,0:T(8,128)(2,1)S(1)} %bitcast.10, bf16[4,2048,512]{2,1,0:T(8,128)(2,1)S(1)} %copy-done, s32[1,256]{1,0:T(1,128)S(1)} %bitcast.12, s32[1,256]{1,0:T(1,128)S(1)} %bitcast.14, s32[1,256]{1,0:T(1,128)S(1)} %bitcast.16, ...), custom_call_target="tpu_custom_call" | custom-call | tf_op jit(solution)/shard_map/pallas_call | solution.py:94
  14.7 53.1 %shard_map.103 = f32[128,1024]{1,0:T(8,128)S(1)} custom-call(f32[16,96,128]{2,1,0:T(8,128)S(1)} %get-tuple-element.7.sums_ref, f32[128,128]{1,0:T(8,128)S(1)} %get-tuple-element.8.gram_ref), custom_call_target="tpu_custom_call" | custom-call | tf_op jit(solution)/shard_map/pallas_call | solution.py:290
  67.9 1.6 %fusion = f32[1,1,256,1024]{3,2,1,0:T(8,128)} fusion(f32[256,1024]{1,0:T(8,128)S(1)} %get-tuple-element.9, f32[128,1024]{1,0:T(8,128)S(1)} %shard_map.103, pred[64,256]{1,0:T(32,128)(4,1)S(1)} %iota_compare_fusion, pred[32,256]{1,0:T(32,128)(4,1)S(1)} %get-tuple-element.12, pred[32,256]{1,0:T(32,128)(4,1)S(1)} %get-tuple-element.13), kind=kOutput, calls=%fused_computation.1 | convolution fusion | flops 402980864 | bytes 2654208 | tf_op jit(solution)/shard_map/dot_general | solution.py:323
  69.5 0.7 %slice.11 = f32[64,1024]{1,0:T(8,128)} slice(f32[128,1024]{1,0:T(8,128)S(1)} %shard_map.103), slice={[64:128], [0:1024]} | slice | bytes 524288 | tf_op jit(solution)/shard_map/slice | solution.py:327
  70.2 0.7 %fusion.7 = (f32[32,1024]{1,0:T(8,128)}, f32[32,1024]{1,0:T(8,128)}) fusion(f32[128,1024]{1,0:T(8,128)S(1)} %shard_map.103), kind=kLoop, calls=%fused_computation.11 | loop fusion | bytes 524288 | tf_op jit(solution)/shard_map/slice | solution.py:327
Async XLA Ops:
  2.0 3.4 %copy-start = (bf16[4,2048,512]{2,1,0:T(8,128)(2,1)S(1)}, bf16[4,2048,512]{2,1,0:T(8,128)(2,1)}, u32[]{:S(2)}) copy-start(bf16[4,2048,512]{2,1,0:T(8,128)(2,1)} %constant.2.clone.tables_ref) | copy-start | bytes 25165828
  5.4 1.2 %copy-start.1 = (bf16[1,1,256,2048]{3,2,1,0:T(8,128)(2,1)S(1)}, bf16[1,1,256,2048]{3,2,1,0:T(8,128)(2,1)}, u32[]{:S(2)}) copy-start(bf16[1,1,256,2048]{3,2,1,0:T(8,128)(2,1)} %param.7) | copy-start | bytes 3145732
  6.7 0.9 %copy-start.2 = (f32[64,1024]{1,0:T(8,128)S(1)}, f32[64,1024]{1,0:T(8,128)}, u32[]{:S(2)}) copy-start(f32[64,1024]{1,0:T(8,128)} %oinit_ref.1) | copy-start | bytes 786436
  7.6 0.9 %copy-start.3 = (f32[32,1024]{1,0:T(8,128)S(1)}, f32[32,1024]{1,0:T(8,128)}, u32[]{:S(2)}) copy-start(f32[32,1024]{1,0:T(8,128)} %rinit_ref.1) | copy-start | bytes 393220
  8.5 0.7 copy-start.4
  9.2 0.7 copy-start.5
  9.9 0.7 copy-start.6

commit v2 on v0

v2 whole, which is shorter than its diff:
```python
import functools

import jax
import jax.numpy as jnp
import ml_dtypes
import numpy as np
from jax import lax
from jax.experimental import pallas as pl
from jax.experimental.pallas import tpu as pltpu
from jax.sharding import PartitionSpec as P

NSRC = 32
NRCV = 32
NOFF = 64
ROWS = NSRC + NRCV + NOFF
MESH = pl.DeviceIdType.MESH
HIGHEST = lax.Precision.HIGHEST


def dft_tables(samples, bins, chunks):
    times = np.arange(samples, dtype=np.int64)[:, None]
    freqs = np.arange(bins, dtype=np.int64)[None, :]
    phase = (times * freqs) % samples
    angle = phase.astype(np.float32) * np.float32(2.0 * 3.141592653589793 / samples)
    cosine = np.cos(angle).astype(ml_dtypes.bfloat16)
    sine = (-np.sin(angle)).astype(ml_dtypes.bfloat16)
    width = bins // chunks
    return np.stack(
        [
            np.concatenate([t[:, c * width : (c + 1) * width] for t in (cosine, sine)], axis=1)
            for c in range(chunks)
        ]
    )


def hot_rows(src, rcv, off):
    parts = []
    for ids, count in ((src, NSRC), (rcv, NRCV), (off, NOFF)):
        rows = lax.broadcasted_iota(jnp.int32, (count, ids.shape[1]), 0)
        parts.append((rows == ids).astype(jnp.float32))
    return jnp.concatenate(parts, axis=0)


def split(values):
    high = values.astype(jnp.bfloat16)
    low = (values - high.astype(jnp.float32)).astype(jnp.bfloat16)
    return high, low


def dot(a, b):
    return jnp.dot(a, b, preferred_element_type=jnp.float32)


def tiles_of(values, count):
    return [values[:, t * ROWS : (t + 1) * ROWS] for t in range(count)]


def pick(tiles, lane):
    out = pltpu.roll(tiles[0], ROWS - 32, 1)
    out = jnp.where(lane < 32, out, tiles[1])
    out = jnp.where(lane < 64, out, pltpu.roll(tiles[2], 32, 1))
    return jnp.where(lane < 96, out, pltpu.roll(tiles[3], 64, 1))


def sweep_kernel(
    nj, ny, nz, chunks,
    traces_hbm, tables_hbm, src_hbm, rcv_hbm, off_hbm, rinit_hbm, oinit_hbm,
    spectra_hbm, terms_ref, hot_ref,
    traces_buf, tables_buf, ids_buf, init_buf, x_buf, sums_buf,
    gy_buf, gs_buf, gz_buf, gr_buf, a_buf, p_buf, b1_buf, b2_buf, c_buf, d_out, d_buf,
    load_sem, table_sem, store_sem, send_sem, recv_sem,
):
    i = lax.axis_index("src")
    j = lax.axis_index("rcv")
    y = i // nz
    z = lax.rem(i, nz)
    samples = traces_buf.shape[1]
    width = x_buf.shape[2]
    per = a_buf.shape[1]
    few = per // ny
    tiles = nj * NRCV // ROWS
    each = nj // chunks
    first = j // each

    loads = [
        pltpu.make_async_copy(src_hbm, ids_buf.at[0], load_sem.at[0]),
        pltpu.make_async_copy(rcv_hbm, ids_buf.at[1], load_sem.at[1]),
        pltpu.make_async_copy(off_hbm, ids_buf.at[2], load_sem.at[2]),
        pltpu.make_async_copy(traces_hbm, traces_buf, load_sem.at[3]),
        pltpu.make_async_copy(rinit_hbm, init_buf.at[pl.ds(0, NRCV)], load_sem.at[4]),
        pltpu.make_async_copy(oinit_hbm, init_buf.at[pl.ds(NRCV, NOFF)], load_sem.at[5]),
    ]
    order = [lax.rem(first + k, chunks) for k in range(chunks)]
    tables = [
        pltpu.make_async_copy(tables_hbm.at[c], tables_buf.at[c], table_sem.at[k])
        for k, c in enumerate(order)
    ]
    for copy in loads[:4] + tables[:1] + loads[4:] + tables[1:]:
        copy.start()

    def over_j(d):
        peer = lax.rem(j + d, nj)
        return peer, (i, peer)

    def over_y(d):
        peer = lax.rem(y + d, ny)
        return peer, (peer * nz + z, j)

    def over_z(d):
        peer = lax.rem(z + d, nz)
        return peer, (y * nz + peer, j)

    def copy_to(device, source, target, phase):
        return pltpu.make_async_remote_copy(
            src_ref=source, dst_ref=target, send_sem=send_sem.at[phase],
            recv_sem=recv_sem.at[phase], device_id=device, device_id_type=MESH,
        )

    def send(n, over, me, source, buf, phase):
        for d in range(1, n):
            peer, device = over(d)
            copy_to(device, source(peer), buf.at[me], phase).start()

    def all_of(n, over, buf, phase):
        part = buf.at[pl.ds(0, n - 1)]
        return copy_to(over(1)[1], part, part, phase)

    barrier = pltpu.get_barrier_semaphore()
    for n, over in ((ny, over_y), (nj, over_j), (nz, over_z)):
        for d in range(1, n):
            pl.semaphore_signal(barrier, inc=1, device_id=over(d)[1], device_id_type=MESH)

    for copy in loads[:3]:
        copy.wait()
    hot = hot_rows(ids_buf[0], ids_buf[1], ids_buf[2])
    hot_ref[...] = hot.T.astype(jnp.bfloat16)
    hot = hot.astype(jnp.bfloat16)
    gram = lax.dot_general(hot, hot, (((1,), (1,)), ((), ())), preferred_element_type=jnp.float32)
    gy_buf[y] = gram[NSRC : NSRC + NRCV]
    gs_buf[j] = gram[:NSRC]
    row = lax.broadcasted_iota(jnp.int32, (ROWS, ROWS), 0)
    lane = lax.broadcasted_iota(jnp.int32, (ROWS, ROWS), 1)
    from_rcv = (lane >= NSRC) & (lane < NSRC + NRCV) & (row < NSRC)
    from_off = (lane >= NSRC + NRCV) & (row < NSRC + NRCV)
    before = jnp.where(from_rcv | from_off, gram, 0.0).astype(jnp.bfloat16)[:, NSRC:]
    pl.semaphore_wait(barrier, nj + ny + nz - 3)
    send(ny, over_y, y, lambda p: gy_buf.at[y], gy_buf, 0)
    send(nj, over_j, j, lambda p: gs_buf.at[j], gs_buf, 1)

    for copy in loads[3:]:
        copy.wait()
    stores = []
    for k, c in enumerate(order):
        tables[k].wait()
        both = dot(traces_buf[...], tables_buf[c])
        real, imag = both[:, :width], both[:, width:]
        spectra = 0.5 * jnp.log((real * real + imag * imag) * (1.0 / samples) + 0.25)
        x_buf[c] = spectra
        store = pltpu.make_async_copy(x_buf.at[c], spectra_hbm.at[c], store_sem.at[k])
        store.start()
        stores.append(store)
        init = init_buf[:, pl.ds(pl.multiple_of(c * width, width), width)]
        spec_high, spec_low = split(spectra)
        init_high, init_low = split(init)
        sums = (dot(hot, spec_high) - dot(before, init_high)) + (
            dot(hot, spec_low) - dot(before, init_low)
        )
        turned = sums.T
        for q in range(each):
            sums_buf[c * each + q] = turned[q * per : (q + 1) * per]
        for q in range(1 if k == 0 else 0, each):
            peer = c * each + (lax.rem(j + q, each) if k == 0 else q)
            copy_to((i, peer), sums_buf.at[peer], a_buf.at[j], 2).start()
    a_buf[j] = sums_buf[j]

    all_of(ny, over_y, gy_buf, 0).wait_recv()
    gz_buf[z] = jnp.sum(gy_buf[...], axis=0)
    send(nz, over_z, z, lambda p: gz_buf.at[z], gz_buf, 3)
    all_of(nj, over_j, gs_buf, 1).wait_recv()
    lane = lax.broadcasted_iota(jnp.int32, (per, ROWS), 1)
    by_src = [gs_buf[q] for q in range(nj)]
    src_count = functools.reduce(lambda a, b: a + b, by_src)
    n_src = jnp.sum(src_count, axis=0, keepdims=True) + 1.0
    off_high, off_low = split(src_count)
    counts = [
        pick(by_src[4 * t : 4 * t + 4], lane[:NSRC]).astype(jnp.bfloat16) for t in range(tiles)
    ]
    counts = jnp.concatenate(counts + [off_high, off_low], axis=1)
    all_of(nz, over_z, gz_buf, 3).wait_recv()
    gr_buf[j] = jnp.sum(gz_buf[...], axis=0)
    send(nj, over_j, j, lambda p: gr_buf.at[j], gr_buf, 4)

    all_of(nj, over_j, a_buf, 2).wait_recv()
    parts = [a_buf[q] for q in range(nj)]
    total = functools.reduce(lambda a, b: a + b, parts)
    src_terms = jnp.where(lane < NSRC, total / n_src, 0.0)
    both = dot(jnp.concatenate(split(src_terms[:, :NSRC]), axis=0), counts)
    along = tiles_of(both[:per] + both[per:], tiles + 2)
    for t in range(tiles):
        left = pick(parts[4 * t : 4 * t + 4], lane) - along[t]
        p_buf[:, :, t * ROWS : (t + 1) * ROWS] = left.reshape(ny, few, ROWS)
    left = total - along[tiles] - along[tiles + 1]
    p_buf[:, :, tiles * ROWS :] = left.reshape(ny, few, ROWS)
    send(ny, over_y, y, lambda p: p_buf.at[p], b1_buf, 5)
    b1_buf[y] = p_buf[y]

    all_of(nj, over_j, gr_buf, 4).wait_recv()
    by_rcv = gr_buf[...]
    columns = [jnp.sum(by_rcv[q], axis=0, keepdims=True) for q in range(nj)]
    n_off = functools.reduce(lambda a, b: a + b, columns) + 1.0
    columns = [jnp.broadcast_to(c, (few, ROWS)) for c in columns]
    n_rcv = [pick(columns[4 * t : 4 * t + 4], lane[:few]) for t in range(tiles)]
    n_rcv = jnp.concatenate(n_rcv, axis=1) + 1.0
    by_rcv = jnp.concatenate(split(by_rcv.reshape(nj * NRCV, ROWS)), axis=1)

    all_of(ny, over_y, b1_buf, 5).wait_recv()
    b2_buf[z] = jnp.sum(b1_buf[...], axis=0)
    send(nz, over_z, z, lambda p: b2_buf.at[z], b2_buf, 6)
    all_of(nz, over_z, b2_buf, 6).wait_recv()

    reduced = b2_buf[0]
    for q in range(1, nz):
        reduced = reduced + b2_buf[q]
    rcv_terms = reduced[:, : tiles * ROWS] / n_rcv
    both = dot(jnp.concatenate(split(rcv_terms), axis=0), by_rcv)
    both = both[:few] + both[few:]
    later = reduced[:, tiles * ROWS :] - both[:, :ROWS] - both[:, ROWS:]
    c_buf[y] = jnp.concatenate([rcv_terms, later / n_off], axis=1)
    send(ny, over_y, y, lambda p: c_buf.at[y], c_buf, 7)
    all_of(ny, over_y, c_buf, 7).wait_recv()

    off_tile = c_buf[:, :, tiles * ROWS :].reshape(per, ROWS)
    for t in range(tiles):
        tile = c_buf[:, :, t * ROWS : (t + 1) * ROWS].reshape(per, ROWS)
        for q in range(4):
            turned = tile if q == 1 else pltpu.roll(tile, (32 - 32 * q) % ROWS, 1)
            d_out[4 * t + q] = jnp.where(
                lane < NSRC, src_terms, jnp.where(lane < NSRC + NRCV, turned, off_tile)
            )
    send(nj, over_j, j, lambda p: d_out.at[p], d_buf, 8)
    d_buf[j] = d_out[j]
    for phase, (n, over, buf) in enumerate((
        (ny, over_y, gy_buf), (nj, over_j, gs_buf), (nj, over_j, a_buf), (nz, over_z, gz_buf),
        (nj, over_j, gr_buf), (ny, over_y, b1_buf), (nz, over_z, b2_buf), (ny, over_y, c_buf),
        (nj, over_j, d_buf),
    )):
        all_of(n, over, buf, phase).wait_send()
    for store in stores:
        store.wait()
    all_of(nj, over_j, d_buf, 8).wait_recv()
    terms_ref[...] = d_buf[...].reshape(nj * per, ROWS)


def sweep(traces, src, rcv, off, receiver_init, offset_init, nj, ny, nz):
    traces_n, samples = traces.shape
    bins = receiver_init.shape[1]
    chunks = max(1, bins // 256)
    width = bins // chunks
    per = bins // nj
    few = per // ny
    wide = nj * NRCV + ROWS
    f32, b16 = jnp.float32, jnp.bfloat16
    tables = jnp.asarray(dft_tables(samples, bins, chunks))
    hbm = pl.BlockSpec(memory_space=pltpu.HBM)
    dma = pltpu.SemaphoreType.DMA
    return pl.pallas_call(
        functools.partial(sweep_kernel, nj, ny, nz, chunks),
        in_specs=[hbm] * 7,
        out_specs=[pl.BlockSpec(memory_space=pl.ANY)] + [pl.BlockSpec(memory_space=pltpu.VMEM)] * 2,
        out_shape=[
            jax.ShapeDtypeStruct((chunks, traces_n, width), f32),
            jax.ShapeDtypeStruct((bins, ROWS), f32),
            jax.ShapeDtypeStruct((traces_n, ROWS), b16),
        ],
        scratch_shapes=[
            pltpu.VMEM((traces_n, samples), b16),
            pltpu.VMEM((chunks, samples, 2 * width), b16),
            pltpu.VMEM((3, 1, traces_n), jnp.int32),
            pltpu.VMEM((NRCV + NOFF, bins), f32),
            pltpu.VMEM((chunks, traces_n, width), f32),
            pltpu.VMEM((nj, per, ROWS), f32),
            pltpu.VMEM((ny, NRCV, ROWS), f32),
            pltpu.VMEM((nj, NSRC, ROWS), f32),
            pltpu.VMEM((nz, NRCV, ROWS), f32),
            pltpu.VMEM((nj, NRCV, ROWS), f32),
            pltpu.VMEM((nj, per, ROWS), f32),
            pltpu.VMEM((ny, few, wide), f32),
            pltpu.VMEM((ny, few, wide), f32),
            pltpu.VMEM((nz, few, wide), f32),
            pltpu.VMEM((ny, few, wide), f32),
            pltpu.VMEM((nj, per, ROWS), f32),
            pltpu.VMEM((nj, per, ROWS), f32),
            dma((6,)), dma((chunks,)), dma((chunks,)), dma((9,)), dma((9,)),
        ],
        compiler_params=pltpu.CompilerParams(
            collective_id=0, has_side_effects=True, vmem_limit_bytes=60 * 1024 * 1024
        ),
    )(traces, tables, src, rcv, off, receiver_init, offset_init)


def finish_kernel(
    hot_ref, spectra_ref, turned_ref, src_out, rcv_out, off_out, residual_ref
):
    hot = hot_ref[...]
    turned = turned_ref[...]
    high, low = split(turned)
    over_lanes = (((1,), (1,)), ((), ()))
    spread = lax.dot_general(hot, high, over_lanes, preferred_element_type=jnp.float32)
    spread += lax.dot_general(hot, low, over_lanes, preferred_element_type=jnp.float32)
    residual_ref[0, 0] = spectra_ref[0] - spread
    terms = turned.T
    src_out[...] = terms[:NSRC]
    rcv_out[...] = terms[NSRC : NSRC + NRCV]
    off_out[...] = terms[NSRC + NRCV :]


def finish(hot, spectra, turned):
    chunks, traces_n, width = spectra.shape
    bins = chunks * width
    whole = lambda c: (0, 0)
    along = lambda c: (0, c)
    f32 = jnp.float32
    return pl.pallas_call(
        finish_kernel,
        grid=(chunks,),
        in_specs=[
            pl.BlockSpec((traces_n, ROWS), whole),
            pl.BlockSpec((1, traces_n, width), lambda c: (c, 0, 0)),
            pl.BlockSpec((width, ROWS), lambda c: (c, 0)),
        ],
        out_specs=[
            pl.BlockSpec((NSRC, width), along),
            pl.BlockSpec((NRCV, width), along),
            pl.BlockSpec((NOFF, width), along),
            pl.BlockSpec((1, 1, traces_n, width), lambda c: (0, 0, 0, c)),
        ],
        out_shape=[
            jax.ShapeDtypeStruct((NSRC, bins), f32),
            jax.ShapeDtypeStruct((NRCV, bins), f32),
            jax.ShapeDtypeStruct((NOFF, bins), f32),
            jax.ShapeDtypeStruct((1, 1, traces_n, bins), f32),
        ],
        compiler_params=pltpu.CompilerParams(
            dimension_semantics=("arbitrary",), vmem_limit_bytes=60 * 1024 * 1024
        ),
    )(hot, spectra, turned)


def on_device(
    nj, ny, nz, traces, source_ids, receiver_ids, offset_ids, receiver_init, offset_init
):
    src, rcv, off = source_ids[0], receiver_ids[0], offset_ids[0]
    spectra, turned, hot = sweep(
        traces[0, 0], src, rcv, off, receiver_init, offset_init, nj, ny, nz
    )
    return finish(hot, spectra, turned)


def solution(mesh):
    nsrc, nj = mesh.shape["src"], mesh.shape["rcv"]
    nz = 4 if nsrc >= 32 else 2
    ny = nsrc // nz
    placed = (
        P("src", "rcv", None, None),
        P("src", "rcv", None),
        P("src", "rcv", None),
        P("src", "rcv", None),
        P("rcv", None),
        P(),
    )
    return jax.shard_map(
        functools.partial(on_device, nj, ny, nz),
        mesh=mesh,
        in_specs=placed,
        out_specs=(P("src", None), P("rcv", None), P(), P("src", "rcv", None, None)),
        check_vma=False,
    )
```

time: 835 us -> 57.7 us (0.07)
  waiting for transfers between devices: 557 us -> 0 us
  blocking collectives: 213 us -> 0 us
  Pallas kernels: 0 us -> 56.9 us
  other arithmetic: 38.1 us -> 0 us
  between operations: 14.1 us -> 0.64 us
  matrix products: 11.3 us -> 0 us
    psum x3 -> x0, waiting for transfers between devices: 556 us -> none  [the longest x1 285 us: on_device(): off_total = lax.psum(collect(off_hot, later), ('src', 'rcv'))]
    psum x3 -> x0, blocking collectives: 213 us -> none  [the longest x1 110 us: on_device(): off_count = lax.psum(jnp.sum(off_hot, axis=1), ('src', 'rcv'))]
    pallas_call x0 -> x2, Pallas kernels: none -> 56.9 us  [the longest x1 53 us: sweep(): pl.pallas_call(functools.partial(sweep_kernel, nj, ny, nz, chunks), in_sp...]
    another operation x4 -> x0, other arithmetic: 34.4 us -> none
    dot_general x12 -> x0, matrix products: 11.3 us -> none  [the longest x5 4.27 us: spread(): jnp.dot(hot.T, terms, precision=lax.Precision.HIGHEST, preferred_element_...]
  transfers between devices with their start and end apart: 3 -> 0, of which waited for: 2 -> 0; matrix products, arithmetic and copies ran while one was open for 0% -> 0% of each run, Pallas kernels for 0% -> 0%
where the time goes in v2:
time: 57.7 us; the launch traced here: 57.5 us
  Pallas kernels  56.9 us (99%)
  between operations  0.64 us (1%)
    pallas_call x1, Pallas kernels, sweep(): pl.pallas_call(functools.partial(sweep_kernel, nj, ny, nz, chunks), in_sp...  53 us
    pallas_call x1, Pallas kernels, finish(): pl.pallas_call(finish_kernel, grid=(chunks,), in_specs=[pl.BlockSpec((tra...  3.9 us

profile of v2, /device:TPU:1, one launch (start us, length us, event | category | flops | bytes accessed | tf_op | source)
XLA Modules:
  0.0 57.5 jit_solution(9784247947082927860)
XLA Ops:
  0.6 53.0 %shard_map.102 = (f32[4,256,256]{2,1,0:T(8,128)}, f32[1024,128]{1,0:T(8,128)}, bf16[256,128]{1,0:T(8,128)(2,1)}) custom-call(bf16[256,2048]{1,0:T(8,128)(2,1)} %bitcast.4, bf16[4,2048,512]{2,1,0:T(8,128)(2,1)} %constant.2.clone.tables_hbm, s32[1,256]{1,0:T(1,128)} %bitcast.5, s32[1,256]{1,0:T(1,128)} %bitcast.6, s32[1,256]{1,0:T(1,128)} %bitcast.7, ...), custom_call_target="tpu_custom_call" | custom-call | tf_op jit(solution)/shard_map/pallas_call | solution.py:266
  53.6 3.9 %shard_map.103 = (f32[32,1024]{1,0:T(8,128)}, f32[32,1024]{1,0:T(8,128)}, f32[64,1024]{1,0:T(8,128)}, f32[1,1,256,1024]{3,2,1,0:T(8,128)}) custom-call(bf16[256,128]{1,0:T(8,128)(2,1)} %get-tuple-element.7.hot_ref, f32[4,256,256]{2,1,0:T(8,128)} %get-tuple-element.8.spectra_ref, f32[1024,128]{1,0:T(8,128)} %get-tuple-element.9.turned_ref), custom_call_target="tpu_custom_call" | custom-call | tf_op jit(solution)/shard_map/pallas_call | solution.py:323

commit v3 on v2

v3 whole, which is shorter than its diff:
```python
import functools

import jax
import jax.numpy as jnp
import ml_dtypes
import numpy as np
from jax import lax
from jax.experimental import pallas as pl
from jax.experimental.pallas import tpu as pltpu
from jax.sharding import PartitionSpec as P

NSRC = 32
NRCV = 32
NOFF = 64
ROWS = NSRC + NRCV + NOFF
MESH = pl.DeviceIdType.MESH
OVER_LANES = (((1,), (1,)), ((), ()))


def dft_tables(samples, bins, chunks):
    times = np.arange(samples, dtype=np.int64)[:, None]
    freqs = np.arange(bins, dtype=np.int64)[None, :]
    phase = (times * freqs) % samples
    angle = phase.astype(np.float32) * np.float32(2.0 * 3.141592653589793 / samples)
    cosine = np.cos(angle).astype(ml_dtypes.bfloat16)
    sine = (-np.sin(angle)).astype(ml_dtypes.bfloat16)
    width = bins // chunks
    return np.stack(
        [
            np.concatenate([t[:, c * width : (c + 1) * width] for t in (cosine, sine)], axis=1)
            for c in range(chunks)
        ]
    )


def hot_rows(src, rcv, off):
    parts = []
    for ids, count in ((src, NSRC), (rcv, NRCV), (off, NOFF)):
        rows = lax.broadcasted_iota(jnp.int32, (count, ids.shape[1]), 0)
        parts.append((rows == ids).astype(jnp.float32))
    return jnp.concatenate(parts, axis=0)


def split(values):
    high = values.astype(jnp.bfloat16)
    low = (values - high.astype(jnp.float32)).astype(jnp.bfloat16)
    return high, low


def dot(a, b):
    return jnp.dot(a, b, preferred_element_type=jnp.float32)


def tiles_of(values, count):
    return [values[:, t * ROWS : (t + 1) * ROWS] for t in range(count)]


def pick(tiles, lane):
    out = pltpu.roll(tiles[0], ROWS - 32, 1)
    out = jnp.where(lane < 32, out, tiles[1])
    out = jnp.where(lane < 64, out, pltpu.roll(tiles[2], 32, 1))
    return jnp.where(lane < 96, out, pltpu.roll(tiles[3], 64, 1))


HALVES = 2


def add(values):
    return functools.reduce(lambda a, b: a + b, values)


def sweep_kernel(
    nj, ny, nz, groups,
    traces_hbm, tables_hbm, src_hbm, rcv_hbm, off_hbm, rinit_hbm, oinit_hbm,
    spectra_hbm, terms_hbm, hot_hbm,
    traces_buf, tables_buf, ids_buf, init_buf, x_buf, hot_buf, sums_buf,
    gy_buf, gz_buf, gr_buf, a_buf, flat_buf, p_buf, b1_buf, b2_buf, c_buf, d_out,
    load_sem, table_sem, store_sem, send_sem, recv_sem,
):
    i = lax.axis_index("src")
    j = lax.axis_index("rcv")
    y = i // nz
    z = lax.rem(i, nz)
    samples = traces_buf.shape[1]
    width = x_buf.shape[2]
    per = a_buf.shape[2]
    few = per // ny
    tiles = nj * NRCV // ROWS
    each = nj // groups
    first = j // each

    mine = ids_buf.at[j]
    loads = [
        pltpu.make_async_copy(src_hbm, mine.at[0], load_sem.at[0]),
        pltpu.make_async_copy(rcv_hbm, mine.at[1], load_sem.at[1]),
        pltpu.make_async_copy(off_hbm, mine.at[2], load_sem.at[2]),
        pltpu.make_async_copy(traces_hbm, traces_buf, load_sem.at[3]),
        pltpu.make_async_copy(rinit_hbm, init_buf.at[pl.ds(0, NRCV)], load_sem.at[4]),
        pltpu.make_async_copy(oinit_hbm, init_buf.at[pl.ds(NRCV, NOFF)], load_sem.at[5]),
    ]
    order = [h * groups + lax.rem(first + k, groups) for h in range(HALVES) for k in range(groups)]
    tables = [
        pltpu.make_async_copy(tables_hbm.at[c], tables_buf.at[c], table_sem.at[k])
        for k, c in enumerate(order)
    ]
    for copy in loads[:4] + tables[:1] + loads[4:] + tables[1:]:
        copy.start()

    def over_j(d):
        peer = lax.rem(j + d, nj)
        return peer, (i, peer)

    def over_y(d):
        peer = lax.rem(y + d, ny)
        return peer, (peer * nz + z, j)

    def over_z(d):
        peer = lax.rem(z + d, nz)
        return peer, (y * nz + peer, j)

    def copy_to(device, source, target, phase):
        return pltpu.make_async_remote_copy(
            src_ref=source, dst_ref=target, send_sem=send_sem.at[phase],
            recv_sem=recv_sem.at[phase], device_id=device, device_id_type=MESH,
        )

    def send(n, over, me, source, buf, phase):
        for d in range(1, n):
            peer, device = over(d)
            copy_to(device, source(peer), buf.at[me], phase).start()

    def all_of(n, over, buf, phase):
        part = buf.at[pl.ds(0, n - 1)]
        return copy_to(over(1)[1], part, part, phase)

    barrier = pltpu.get_barrier_semaphore()
    for n, over in ((ny, over_y), (nj, over_j), (nz, over_z)):
        for d in range(1, n):
            pl.semaphore_signal(barrier, inc=1, device_id=over(d)[1], device_id_type=MESH)

    for copy in loads[:3]:
        copy.wait()
    hot = hot_rows(ids_buf[j, 0], ids_buf[j, 1], ids_buf[j, 2])
    hot_buf[...] = hot.T.astype(jnp.bfloat16)
    hot = hot.astype(jnp.bfloat16)
    gram = lax.dot_general(hot, hot, OVER_LANES, preferred_element_type=jnp.float32)
    gy_buf[y] = gram[NSRC : NSRC + NRCV]
    row = lax.broadcasted_iota(jnp.int32, (ROWS, ROWS), 0)
    lane = lax.broadcasted_iota(jnp.int32, (ROWS, ROWS), 1)
    from_rcv = (lane >= NSRC) & (lane < NSRC + NRCV) & (row < NSRC)
    from_off = (lane >= NSRC + NRCV) & (row < NSRC + NRCV)
    before = jnp.where(from_rcv | from_off, gram, 0.0).astype(jnp.bfloat16)[:, NSRC:]
    pl.semaphore_wait(barrier, nj + ny + nz - 3)
    send(nj, over_j, j, lambda p: ids_buf.at[j], ids_buf, 0)
    send(ny, over_y, y, lambda p: gy_buf.at[y], gy_buf, 1)
    stores = [pltpu.make_async_copy(hot_buf, hot_hbm, load_sem.at[0])]
    stores[0].start()

    for copy in loads[3:]:
        copy.wait()
    for n, c in enumerate(order):
        h, k = n // groups, n % groups
        g = c - h * groups
        tables[n].wait()
        both = dot(traces_buf[...], tables_buf[c])
        real, imag = both[:, :width], both[:, width:]
        spectra = 0.5 * jnp.log((real * real + imag * imag) * (1.0 / samples) + 0.25)
        x_buf[c] = spectra
        store = pltpu.make_async_copy(x_buf.at[c], spectra_hbm.at[c], store_sem.at[n])
        store.start()
        stores.append(store)
        init = init_buf[:, pl.ds(pl.multiple_of(c * width, width), width)]
        spec_high, spec_low = split(spectra)
        init_high, init_low = split(init)
        sums = (dot(hot, spec_high) - dot(before, init_high)) + (
            dot(hot, spec_low) - dot(before, init_low)
        )
        turned = sums.T
        for q in range(each):
            sums_buf[h, g * each + q] = turned[q * per : (q + 1) * per]
        for q in range(1 if k == 0 else 0, each):
            peer = g * each + (lax.rem(j + q, each) if k == 0 else q)
            copy_to((i, peer), sums_buf.at[h, peer], a_buf.at[h, j], 4 + 5 * h).start()
    for h in range(HALVES):
        a_buf[h, j] = sums_buf[h, j]

    all_of(ny, over_y, gy_buf, 1).wait_recv()
    gz_buf[z] = jnp.sum(gy_buf[...], axis=0)
    send(nz, over_z, z, lambda p: gz_buf.at[z], gz_buf, 2)
    all_of(nj, over_j, ids_buf, 0).wait_recv()
    by_src = []
    for q in range(nj):
        peer_hot = hot_rows(ids_buf[q, 0], ids_buf[q, 1], ids_buf[q, 2]).astype(jnp.bfloat16)
        by_src.append(
            lax.dot_general(
                peer_hot[:NSRC], peer_hot, OVER_LANES, preferred_element_type=jnp.float32
            )
        )
    src_count = add(by_src)
    n_src = jnp.sum(src_count, axis=0, keepdims=True) + 1.0
    off_high, off_low = split(src_count)
    counts = [
        pick(by_src[4 * t : 4 * t + 4], lane[:NSRC]).astype(jnp.bfloat16) for t in range(tiles)
    ]
    counts = jnp.concatenate(counts + [off_high, off_low], axis=1)
    lane = lane[:per]

    def source_step(h):
        all_of(nj, over_j, a_buf.at[h], 4 + 5 * h).wait_recv()
        parts = [a_buf[h, q] for q in range(nj)]
        total = add(parts)
        src_terms = jnp.where(lane < NSRC, total / n_src, 0.0)
        both = dot(jnp.concatenate(split(src_terms[:, :NSRC]), axis=0), counts)
        along = tiles_of(both[:per] + both[per:], tiles + 2)
        for t in range(tiles):
            left = pick(parts[4 * t : 4 * t + 4], lane) - along[t]
            flat_buf[h, :, t * ROWS : (t + 1) * ROWS] = left
        flat_buf[h, :, tiles * ROWS :] = total - along[tiles] - along[tiles + 1]
        for q in range(ny):
            p_buf[h, q] = flat_buf[h, q * few : (q + 1) * few, :]
        send(ny, over_y, y, lambda p: p_buf.at[h, p], b1_buf.at[h], 5 + 5 * h)
        b1_buf[h, y] = p_buf[h, y]
        return src_terms

    def reduce_step(h):
        all_of(ny, over_y, b1_buf.at[h], 5 + 5 * h).wait_recv()
        b2_buf[h, z] = add([b1_buf[h, q] for q in range(ny)])
        send(nz, over_z, z, lambda p: b2_buf.at[h, z], b2_buf.at[h], 6 + 5 * h)

    def term_step(h):
        all_of(nz, over_z, b2_buf.at[h], 6 + 5 * h).wait_recv()
        reduced = add([b2_buf[h, q] for q in range(nz)])
        rcv_terms = reduced[:, : tiles * ROWS] / n_rcv
        high, low = split(rcv_terms)
        both = dot(high, by_rcv) + dot(low, by_rcv)
        later = reduced[:, tiles * ROWS :] - both[:, :ROWS] - both[:, ROWS:]
        c_buf[h, y] = jnp.concatenate([rcv_terms, later / n_off], axis=1)
        send(ny, over_y, y, lambda p: c_buf.at[h, y], c_buf.at[h], 7 + 5 * h)

    def back_step(h, src_terms):
        all_of(ny, over_y, c_buf.at[h], 7 + 5 * h).wait_recv()
        for q in range(ny):
            flat_buf[h, q * few : (q + 1) * few, :] = c_buf[h, q]
        off_tile = flat_buf[h, :, tiles * ROWS :]
        for t in range(tiles):
            tile = flat_buf[h, :, t * ROWS : (t + 1) * ROWS]
            for q in range(4):
                turned = tile if q == 1 else pltpu.roll(tile, (32 - 32 * q) % ROWS, 1)
                d_out[h, 4 * t + q] = jnp.where(
                    lane < NSRC, src_terms, jnp.where(lane < NSRC + NRCV, turned, off_tile)
                )
        send(nj, over_j, j, lambda p: d_out.at[h, p], terms_hbm.at[h], 8 + 5 * h)
        own = pltpu.make_async_copy(d_out.at[h, j], terms_hbm.at[h, j], load_sem.at[1 + h])
        own.start()
        stores.append(own)

    src_low = source_step(0)
    all_of(nz, over_z, gz_buf, 2).wait_recv()
    gr_buf[j] = jnp.sum(gz_buf[...], axis=0)
    send(nj, over_j, j, lambda p: gr_buf.at[j], gr_buf, 3)
    src_high = source_step(1)
    reduce_step(0)

    all_of(nj, over_j, gr_buf, 3).wait_recv()
    by_rcv = gr_buf[...]
    columns = [jnp.sum(by_rcv[q], axis=0, keepdims=True) for q in range(nj)]
    n_off = add(columns) + 1.0
    columns = [jnp.broadcast_to(c, (8, ROWS)) for c in columns]
    n_rcv = [pick(columns[4 * t : 4 * t + 4], lane[:8])[:1] for t in range(tiles)]
    n_rcv = jnp.concatenate(n_rcv, axis=1) + 1.0
    by_rcv = jnp.concatenate(split(by_rcv.reshape(nj * NRCV, ROWS)), axis=1)

    term_step(0)
    reduce_step(1)
    back_step(0, src_low)
    term_step(1)
    back_step(1, src_high)

    for phase, (n, over, buf) in enumerate(
        [(nj, over_j, ids_buf), (ny, over_y, gy_buf), (nz, over_z, gz_buf), (nj, over_j, gr_buf)]
    ):
        all_of(n, over, buf, phase).wait_send()
    for h in range(HALVES):
        for phase, (n, over, buf) in enumerate(
            [
                (nj, over_j, a_buf), (ny, over_y, b1_buf), (nz, over_z, b2_buf),
                (ny, over_y, c_buf), (nj, over_j, d_out),
            ]
        ):
            all_of(n, over, buf.at[h], 4 + 5 * h + phase).wait_send()
    for store in stores:
        store.wait()
    for h in range(HALVES):
        all_of(nj, over_j, terms_hbm.at[h], 8 + 5 * h).wait_recv()


def sweep(traces, src, rcv, off, receiver_init, offset_init, nj, ny, nz):
    traces_n, samples = traces.shape
    bins = receiver_init.shape[1]
    groups = max(1, bins // (256 * HALVES))
    chunks = HALVES * groups
    width = bins // chunks
    per = bins // nj // HALVES
    few = per // ny
    wide = nj * NRCV + ROWS
    f32, b16 = jnp.float32, jnp.bfloat16
    tables = jnp.asarray(dft_tables(samples, bins, chunks))
    anywhere = pl.BlockSpec(memory_space=pl.ANY)
    dma = pltpu.SemaphoreType.DMA
    phases = 4 + 5 * HALVES
    return pl.pallas_call(
        functools.partial(sweep_kernel, nj, ny, nz, groups),
        in_specs=[anywhere] * 7,
        out_specs=[anywhere] * 3,
        out_shape=[
            jax.ShapeDtypeStruct((chunks, traces_n, width), f32),
            jax.ShapeDtypeStruct((HALVES, nj, per, ROWS), f32),
            jax.ShapeDtypeStruct((traces_n, ROWS), b16),
        ],
        scratch_shapes=[
            pltpu.VMEM((traces_n, samples), b16),
            pltpu.VMEM((chunks, samples, 2 * width), b16),
            pltpu.VMEM((nj, 3, 1, traces_n), jnp.int32),
            pltpu.VMEM((NRCV + NOFF, bins), f32),
            pltpu.VMEM((chunks, traces_n, width), f32),
            pltpu.VMEM((traces_n, ROWS), b16),
            pltpu.VMEM((HALVES, nj, per, ROWS), f32),
            pltpu.VMEM((ny, NRCV, ROWS), f32),
            pltpu.VMEM((nz, NRCV, ROWS), f32),
            pltpu.VMEM((nj, NRCV, ROWS), f32),
            pltpu.VMEM((HALVES, nj, per, ROWS), f32),
            pltpu.VMEM((HALVES, per, wide), f32),
            pltpu.VMEM((HALVES, ny, few, wide), f32),
            pltpu.VMEM((HALVES, ny, few, wide), f32),
            pltpu.VMEM((HALVES, nz, few, wide), f32),
            pltpu.VMEM((HALVES, ny, few, wide), f32),
            pltpu.VMEM((HALVES, nj, per, ROWS), f32),
            dma((6,)), dma((chunks,)), dma((chunks,)), dma((phases,)), dma((phases,)),
        ],
        compiler_params=pltpu.CompilerParams(
            collective_id=0, has_side_effects=True, vmem_limit_bytes=60 * 1024 * 1024
        ),
    )(traces, tables, src, rcv, off, receiver_init, offset_init)


def finish_kernel(
    hot_hbm, spectra_hbm, turned_hbm, src_out, rcv_out, off_out, residual_out,
    hot_buf, x_buf, turned_buf, terms_buf, load_sem, x_sem, turned_sem, store_sem, out_sem,
):
    chunks, _, width = x_buf.shape
    load = pltpu.make_async_copy(hot_hbm, hot_buf, load_sem.at[0])
    load.start()
    parts = []
    for c in range(chunks):
        rows = pl.ds(c * width, width)
        parts.append((
            pltpu.make_async_copy(turned_hbm.at[rows], turned_buf.at[rows], turned_sem.at[c]),
            pltpu.make_async_copy(spectra_hbm.at[c], x_buf.at[c], x_sem.at[c]),
        ))
        for copy in parts[c]:
            copy.start()
    load.wait()
    hot = hot_buf[...]
    stores = []
    for c in range(chunks):
        for copy in parts[c]:
            copy.wait()
        span = slice(c * width, (c + 1) * width)
        turned = turned_buf[span]
        high, low = split(turned)
        spread = lax.dot_general(hot, high, OVER_LANES, preferred_element_type=jnp.float32)
        spread += lax.dot_general(hot, low, OVER_LANES, preferred_element_type=jnp.float32)
        x_buf[c] = x_buf[c] - spread
        store = pltpu.make_async_copy(
            x_buf.at[c], residual_out.at[0, 0, :, pl.ds(c * width, width)], store_sem.at[c]
        )
        store.start()
        stores.append(store)
        terms_buf[:, span] = turned.T
    start = 0
    for k, (out, count) in enumerate(((src_out, NSRC), (rcv_out, NRCV), (off_out, NOFF))):
        store = pltpu.make_async_copy(terms_buf.at[pl.ds(start, count)], out, out_sem.at[k])
        store.start()
        stores.append(store)
        start += count
    for store in stores:
        store.wait()


def finish(hot, spectra, turned):
    chunks, traces_n, width = spectra.shape
    bins = chunks * width
    f32 = jnp.float32
    anywhere = pl.BlockSpec(memory_space=pl.ANY)
    dma = pltpu.SemaphoreType.DMA
    return pl.pallas_call(
        finish_kernel,
        in_specs=[anywhere] * 3,
        out_specs=[anywhere] * 4,
        out_shape=[
            jax.ShapeDtypeStruct((NSRC, bins), f32),
            jax.ShapeDtypeStruct((NRCV, bins), f32),
            jax.ShapeDtypeStruct((NOFF, bins), f32),
            jax.ShapeDtypeStruct((1, 1, traces_n, bins), f32),
        ],
        scratch_shapes=[
            pltpu.VMEM(hot.shape, hot.dtype),
            pltpu.VMEM(spectra.shape, f32),
            pltpu.VMEM(turned.shape, f32),
            pltpu.VMEM((ROWS, bins), f32),
            dma((1,)), dma((chunks,)), dma((chunks,)), dma((chunks,)), dma((3,)),
        ],
        compiler_params=pltpu.CompilerParams(vmem_limit_bytes=60 * 1024 * 1024),
    )(hot, spectra, turned)


def on_device(
    nj, ny, nz, traces, source_ids, receiver_ids, offset_ids, receiver_init, offset_init
):
    src, rcv, off = source_ids[0], receiver_ids[0], offset_ids[0]
    spectra, turned, hot = sweep(
        traces[0, 0], src, rcv, off, receiver_init, offset_init, nj, ny, nz
    )
    return finish(hot, spectra, turned.reshape(-1, ROWS))


def solution(mesh):
    nsrc, nj = mesh.shape["src"], mesh.shape["rcv"]
    nz = 4 if nsrc >= 32 else 2
    ny = nsrc // nz
    placed = (
        P("src", "rcv", None, None),
        P("src", "rcv", None),
        P("src", "rcv", None),
        P("src", "rcv", None),
        P("rcv", None),
        P(),
    )
    return jax.shard_map(
        functools.partial(on_device, nj, ny, nz),
        mesh=mesh,
        in_specs=placed,
        out_specs=(P("src", None), P("rcv", None), P(), P("src", "rcv", None, None)),
        check_vma=False,
    )
```

time: 57.7 us -> 54 us (0.936)
  Pallas kernels: 56.9 us -> 53.2 us
    pallas_call x2, Pallas kernels: 56.9 us -> 53.2 us  [the longest x1 49.9 us: sweep(): pl.pallas_call(functools.partial(sweep_kernel, nj, ny, nz, groups), in_sp...]
where the time goes in v3:
time: 54 us; the launch traced here: 53.9 us
  Pallas kernels  53.2 us (99%)
  between operations  0.64 us (1%)
    pallas_call x1, Pallas kernels, sweep(): pl.pallas_call(functools.partial(sweep_kernel, nj, ny, nz, groups), in_sp...  49.9 us
    pallas_call x1, Pallas kernels, finish(): pl.pallas_call(finish_kernel, in_specs=[anywhere] * 3, out_specs=[anywher...  3.33 us

profile of v3, /device:TPU:1, one launch (start us, length us, event | category | flops | bytes accessed | tf_op | source)
XLA Modules:
  0.0 53.9 jit_solution(5796491365931773776)
XLA Ops:
  0.6 49.9 %shard_map.102 = (f32[4,256,256]{2,1,0:T(8,128)}, f32[2,16,32,128]{3,2,1,0:T(8,128)}, bf16[256,128]{1,0:T(8,128)(2,1)}) custom-call(bf16[256,2048]{1,0:T(8,128)(2,1)} %bitcast.5, bf16[4,2048,512]{2,1,0:T(8,128)(2,1)} %constant.2.clone.tables_hbm, s32[1,256]{1,0:T(1,128)} %bitcast.7, s32[1,256]{1,0:T(1,128)} %bitcast.8, s32[1,256]{1,0:T(1,128)} %bitcast.9, ...), custom_call_target="tpu_custom_call" | custom-call | tf_op jit(solution)/shard_map/pallas_call | solution.py:311
  50.5 3.3 %shard_map.103 = (f32[32,1024]{1,0:T(8,128)}, f32[32,1024]{1,0:T(8,128)}, f32[64,1024]{1,0:T(8,128)}, f32[1,1,256,1024]{3,2,1,0:T(8,128)}) custom-call(bf16[256,128]{1,0:T(8,128)(2,1)} %get-tuple-element.7.hot_hbm, f32[4,256,256]{2,1,0:T(8,128)} %get-tuple-element.8.spectra_hbm, f32[1024,128]{1,0:T(8,128)} %bitcast.6), custom_call_target="tpu_custom_call" | custom-call | tf_op jit(solution)/shard_map/pallas_call | solution.py:396

commit v4 on v3

--- a/solution.py
+++ b/solution.py
@@ -152,7 +152,6 @@
     before = jnp.where(from_rcv | from_off, gram, 0.0).astype(jnp.bfloat16)[:, NSRC:]
     pl.semaphore_wait(barrier, nj + ny + nz - 3)
     send(nj, over_j, j, lambda p: ids_buf.at[j], ids_buf, 0)
-    send(ny, over_y, y, lambda p: gy_buf.at[y], gy_buf, 1)
     stores = [pltpu.make_async_copy(hot_buf, hot_hbm, load_sem.at[0])]
     stores[0].start()
 
@@ -181,12 +180,11 @@
         for q in range(1 if k == 0 else 0, each):
             peer = g * each + (lax.rem(j + q, each) if k == 0 else q)
             copy_to((i, peer), sums_buf.at[h, peer], a_buf.at[h, j], 4 + 5 * h).start()
+        if n == groups - 1:
+            send(ny, over_y, y, lambda p: gy_buf.at[y], gy_buf, 1)
     for h in range(HALVES):
         a_buf[h, j] = sums_buf[h, j]
 
-    all_of(ny, over_y, gy_buf, 1).wait_recv()
-    gz_buf[z] = jnp.sum(gy_buf[...], axis=0)
-    send(nz, over_z, z, lambda p: gz_buf.at[z], gz_buf, 2)
     all_of(nj, over_j, ids_buf, 0).wait_recv()
     by_src = []
     for q in range(nj):
@@ -204,6 +202,9 @@
     ]
     counts = jnp.concatenate(counts + [off_high, off_low], axis=1)
     lane = lane[:per]
+    all_of(ny, over_y, gy_buf, 1).wait_recv()
+    gz_buf[z] = jnp.sum(gy_buf[...], axis=0)
+    send(nz, over_z, z, lambda p: gz_buf.at[z], gz_buf, 2)
 
     def source_step(h):
         all_of(nj, over_j, a_buf.at[h], 4 + 5 * h).wait_recv()
@@ -255,11 +256,12 @@
         stores.append(own)
 
     src_low = source_step(0)
+    src_high = source_step(1)
     all_of(nz, over_z, gz_buf, 2).wait_recv()
     gr_buf[j] = jnp.sum(gz_buf[...], axis=0)
     send(nj, over_j, j, lambda p: gr_buf.at[j], gr_buf, 3)
-    src_high = source_step(1)
     reduce_step(0)
+    reduce_step(1)
 
     all_of(nj, over_j, gr_buf, 3).wait_recv()
     by_rcv = gr_buf[...]
@@ -271,9 +273,8 @@
     by_rcv = jnp.concatenate(split(by_rcv.reshape(nj * NRCV, ROWS)), axis=1)
 
     term_step(0)
-    reduce_step(1)
+    term_step(1)
     back_step(0, src_low)
-    term_step(1)
     back_step(1, src_high)
 
     for phase, (n, over, buf) in enumerate(

time: 54 us -> 50.9 us (0.943)
  Pallas kernels: 53.2 us -> 50.1 us
    pallas_call x1, Pallas kernels: 49.9 us -> 46.8 us  [sweep(): pl.pallas_call(functools.partial(sweep_kernel, nj, ny, nz, groups), in_sp...]
where the time goes in v4:
time: 50.9 us; the launch traced here: 50.7 us
  Pallas kernels  50.1 us (98%)
  between operations  0.64 us (1%)
    pallas_call x1, Pallas kernels, sweep(): pl.pallas_call(functools.partial(sweep_kernel, nj, ny, nz, groups), in_sp...  46.8 us
    pallas_call x1, Pallas kernels, finish(): pl.pallas_call(finish_kernel, in_specs=[anywhere] * 3, out_specs=[anywher...  3.33 us

profile of v4, /device:TPU:1, one launch (start us, length us, event | category | flops | bytes accessed | tf_op | source)
XLA Modules:
  0.0 50.7 jit_solution(364389340353776653)
XLA Ops:
  0.6 46.8 %shard_map.102 = (f32[4,256,256]{2,1,0:T(8,128)}, f32[2,16,32,128]{3,2,1,0:T(8,128)}, bf16[256,128]{1,0:T(8,128)(2,1)}) custom-call(bf16[256,2048]{1,0:T(8,128)(2,1)} %bitcast.5, bf16[4,2048,512]{2,1,0:T(8,128)(2,1)} %constant.2.clone.tables_hbm, s32[1,256]{1,0:T(1,128)} %bitcast.7, s32[1,256]{1,0:T(1,128)} %bitcast.8, s32[1,256]{1,0:T(1,128)} %bitcast.9, ...), custom_call_target="tpu_custom_call" | custom-call | tf_op jit(solution)/shard_map/pallas_call | solution.py:312
  47.4 3.3 %shard_map.103 = (f32[32,1024]{1,0:T(8,128)}, f32[32,1024]{1,0:T(8,128)}, f32[64,1024]{1,0:T(8,128)}, f32[1,1,256,1024]{3,2,1,0:T(8,128)}) custom-call(bf16[256,128]{1,0:T(8,128)(2,1)} %get-tuple-element.7.hot_hbm, f32[4,256,256]{2,1,0:T(8,128)} %get-tuple-element.8.spectra_hbm, f32[1024,128]{1,0:T(8,128)} %bitcast.6), custom_call_target="tpu_custom_call" | custom-call | tf_op jit(solution)/shard_map/pallas_call | solution.py:397

commit v5 on v4

--- a/solution.py
+++ b/solution.py
@@ -74,7 +74,7 @@
     traces_hbm, tables_hbm, src_hbm, rcv_hbm, off_hbm, rinit_hbm, oinit_hbm,
     spectra_hbm, terms_hbm, hot_hbm,
     traces_buf, tables_buf, ids_buf, init_buf, x_buf, hot_buf, sums_buf,
-    gy_buf, gz_buf, gr_buf, a_buf, flat_buf, p_buf, b1_buf, b2_buf, c_buf, d_out,
+    gy_buf, gz_buf, gr_buf, a_buf, s_buf, flat_buf, p_buf, b1_buf, b2_buf, c_buf, d_out,
     load_sem, table_sem, store_sem, send_sem, recv_sem,
 ):
     i = lax.axis_index("src")
@@ -85,6 +85,7 @@
     width = x_buf.shape[2]
     per = a_buf.shape[2]
     few = per // ny
+    quarter = per // 4
     tiles = nj * NRCV // ROWS
     each = nj // groups
     first = j // each
@@ -221,7 +222,8 @@
             p_buf[h, q] = flat_buf[h, q * few : (q + 1) * few, :]
         send(ny, over_y, y, lambda p: p_buf.at[h, p], b1_buf.at[h], 5 + 5 * h)
         b1_buf[h, y] = p_buf[h, y]
-        return src_terms
+        groups_of = [src_terms[q * quarter : (q + 1) * quarter] for q in range(4)]
+        s_buf[h] = add([groups_of[0]] + [pltpu.roll(groups_of[q], 32 * q, 1) for q in (1, 2, 3)])
 
     def reduce_step(h):
         all_of(ny, over_y, b1_buf.at[h], 5 + 5 * h).wait_recv()
@@ -238,44 +240,75 @@
         c_buf[h, y] = jnp.concatenate([rcv_terms, later / n_off], axis=1)
         send(ny, over_y, y, lambda p: c_buf.at[h, y], c_buf.at[h], 7 + 5 * h)
 
-    def back_step(h, src_terms):
+    def source_out(h):
+        send(
+            nj, over_j, j, lambda p: s_buf.at[h],
+            terms_hbm.at[h, :, pl.ds(3 * quarter, quarter)], 4 + 5 * HALVES + h,
+        )
+        own = pltpu.make_async_copy(
+            s_buf.at[h], terms_hbm.at[h, j, pl.ds(3 * quarter, quarter)], load_sem.at[3 + h]
+        )
+        own.start()
+        stores.append(own)
+
+    def back_step(h):
         all_of(ny, over_y, c_buf.at[h], 7 + 5 * h).wait_recv()
         for q in range(ny):
             flat_buf[h, q * few : (q + 1) * few, :] = c_buf[h, q]
         off_tile = flat_buf[h, :, tiles * ROWS :]
+        off_fill = [pltpu.roll(off_tile[3 * quarter :], shift, 1) for shift in (64, 32)]
         for t in range(tiles):
             tile = flat_buf[h, :, t * ROWS : (t + 1) * ROWS]
             for q in range(4):
                 turned = tile if q == 1 else pltpu.roll(tile, (32 - 32 * q) % ROWS, 1)
-                d_out[h, 4 * t + q] = jnp.where(
-                    lane < NSRC, src_terms, jnp.where(lane < NSRC + NRCV, turned, off_tile)
-                )
-        send(nj, over_j, j, lambda p: d_out.at[h, p], terms_hbm.at[h], 8 + 5 * h)
-        own = pltpu.make_async_copy(d_out.at[h, j], terms_hbm.at[h, j], load_sem.at[1 + h])
+                fill = [pltpu.roll(turned[3 * quarter :], 96, 1)] + off_fill
+                whole = jnp.where(lane < NSRC + NRCV, turned, off_tile)
+                for k in range(3):
+                    rows = slice(k * quarter, (k + 1) * quarter)
+                    d_out[h, 4 * t + q, rows, :] = jnp.where(
+                        lane[:quarter] < 32, fill[k], whole[rows]
+                    )
+        back = terms_hbm.at[h, :, pl.ds(0, 3 * quarter)]
+        send(nj, over_j, j, lambda p: d_out.at[h, p], back, 8 + 5 * h)
+        own = pltpu.make_async_copy(d_out.at[h, j], back.at[j], load_sem.at[1 + h])
         own.start()
         stores.append(own)
 
-    src_low = source_step(0)
-    src_high = source_step(1)
+    source_step(0)
+    source_step(1)
     all_of(nz, over_z, gz_buf, 2).wait_recv()
-    gr_buf[j] = jnp.sum(gz_buf[...], axis=0)
+    count = jnp.sum(gz_buf[...], axis=0)
+    half = NRCV // 2
+    wide = lax.broadcasted_iota(jnp.int32, (half, ROWS), 1) >= NSRC + NRCV
+    gr_buf[j] = jnp.where(wide, count[:half], pltpu.roll(count[half:], ROWS // 2, 1))
     send(nj, over_j, j, lambda p: gr_buf.at[j], gr_buf, 3)
+    for h in range(HALVES):
+        source_out(h)
     reduce_step(0)
     reduce_step(1)
 
     all_of(nj, over_j, gr_buf, 3).wait_recv()
-    by_rcv = gr_buf[...]
-    columns = [jnp.sum(by_rcv[q], axis=0, keepdims=True) for q in range(nj)]
-    n_off = add(columns) + 1.0
-    columns = [jnp.broadcast_to(c, (8, ROWS)) for c in columns]
-    n_rcv = [pick(columns[4 * t : 4 * t + 4], lane[:8])[:1] for t in range(tiles)]
-    n_rcv = jnp.concatenate(n_rcv, axis=1) + 1.0
-    by_rcv = jnp.concatenate(split(by_rcv.reshape(nj * NRCV, ROWS)), axis=1)
+    by_rcv = []
+    for q in range(nj):
+        packed = gr_buf[q]
+        by_rcv.append(jnp.where(wide, packed, 0.0))
+        by_rcv.append(jnp.where(wide, pltpu.roll(packed, ROWS // 2, 1), 0.0))
+    by_rcv = jnp.concatenate(by_rcv, axis=0)
+    n_off = jnp.sum(by_rcv, axis=0, keepdims=True) + 1.0
+    by_rcv = split(by_rcv)
+    ones = jnp.ones((16, ROWS), jnp.bfloat16)
+    n_rcv = add(
+        [
+            lax.dot_general(ones, part, OVER_LANES, preferred_element_type=jnp.float32)
+            for part in by_rcv
+        ]
+    )[:1] + 1.0
+    by_rcv = jnp.concatenate(by_rcv, axis=1)
 
     term_step(0)
     term_step(1)
-    back_step(0, src_low)
-    back_step(1, src_high)
+    back_step(0)
+    back_step(1)
 
     for phase, (n, over, buf) in enumerate(
         [(nj, over_j, ids_buf), (ny, over_y, gy_buf), (nz, over_z, gz_buf), (nj, over_j, gr_buf)]
@@ -289,10 +322,13 @@
             ]
         ):
             all_of(n, over, buf.at[h], 4 + 5 * h + phase).wait_send()
+        sources = terms_hbm.at[h, :, pl.ds(3 * quarter, quarter)]
+        all_of(nj, over_j, sources, 4 + 5 * HALVES + h).wait_send()
+        all_of(nj, over_j, sources, 4 + 5 * HALVES + h).wait_recv()
     for store in stores:
         store.wait()
     for h in range(HALVES):
-        all_of(nj, over_j, terms_hbm.at[h], 8 + 5 * h).wait_recv()
+        all_of(nj, over_j, terms_hbm.at[h, :, pl.ds(0, 3 * quarter)], 8 + 5 * h).wait_recv()
 
 
 def sweep(traces, src, rcv, off, receiver_init, offset_init, nj, ny, nz):
@@ -308,7 +344,7 @@
     tables = jnp.asarray(dft_tables(samples, bins, chunks))
     anywhere = pl.BlockSpec(memory_space=pl.ANY)
     dma = pltpu.SemaphoreType.DMA
-    phases = 4 + 5 * HALVES
+    phases = 4 + 6 * HALVES
     return pl.pallas_call(
         functools.partial(sweep_kernel, nj, ny, nz, groups),
         in_specs=[anywhere] * 7,
@@ -328,14 +364,15 @@
             pltpu.VMEM((HALVES, nj, per, ROWS), f32),
             pltpu.VMEM((ny, NRCV, ROWS), f32),
             pltpu.VMEM((nz, NRCV, ROWS), f32),
-            pltpu.VMEM((nj, NRCV, ROWS), f32),
+            pltpu.VMEM((nj, NRCV // 2, ROWS), f32),
             pltpu.VMEM((HALVES, nj, per, ROWS), f32),
+            pltpu.VMEM((HALVES, per // 4, ROWS), f32),
             pltpu.VMEM((HALVES, per, wide), f32),
             pltpu.VMEM((HALVES, ny, few, wide), f32),
             pltpu.VMEM((HALVES, ny, few, wide), f32),
             pltpu.VMEM((HALVES, nz, few, wide), f32),
             pltpu.VMEM((HALVES, ny, few, wide), f32),
-            pltpu.VMEM((HALVES, nj, per, ROWS), f32),
+            pltpu.VMEM((HALVES, nj, per // 4 * 3, ROWS), f32),
             dma((6,)), dma((chunks,)), dma((chunks,)), dma((phases,)), dma((phases,)),
         ],
         compiler_params=pltpu.CompilerParams(
@@ -344,8 +381,24 @@
     )(traces, tables, src, rcv, off, receiver_init, offset_init)
 
 
+def unpack(packed, per):
+    quarter = per // 4
+    lane = lax.broadcasted_iota(jnp.int32, (quarter, ROWS), 1)
+    out = []
+    for start in range(0, packed.shape[0], per):
+        rows = [packed[start + k * quarter : start + (k + 1) * quarter] for k in range(4)]
+        sources = rows[3]
+        out.append(jnp.where(lane < 32, sources, rows[0]))
+        out.append(jnp.where(lane < 32, pltpu.roll(sources, 96, 1), rows[1]))
+        out.append(jnp.where(lane < 32, pltpu.roll(sources, 64, 1), rows[2]))
+        last = jnp.where(lane < 96, pltpu.roll(rows[1], 64, 1), pltpu.roll(rows[2], 96, 1))
+        last = jnp.where(lane < 64, pltpu.roll(rows[0], 32, 1), last)
+        out.append(jnp.where(lane < 32, pltpu.roll(sources, 32, 1), last))
+    return jnp.concatenate(out, axis=0)
+
+
 def finish_kernel(
-    hot_hbm, spectra_hbm, turned_hbm, src_out, rcv_out, off_out, residual_out,
+    per, hot_hbm, spectra_hbm, turned_hbm, src_out, rcv_out, off_out, residual_out,
     hot_buf, x_buf, turned_buf, terms_buf, load_sem, x_sem, turned_sem, store_sem, out_sem,
 ):
     chunks, _, width = x_buf.shape
@@ -367,7 +420,7 @@
         for copy in parts[c]:
             copy.wait()
         span = slice(c * width, (c + 1) * width)
-        turned = turned_buf[span]
+        turned = unpack(turned_buf[span], per)
         high, low = split(turned)
         spread = lax.dot_general(hot, high, OVER_LANES, preferred_element_type=jnp.float32)
         spread += lax.dot_general(hot, low, OVER_LANES, preferred_element_type=jnp.float32)
@@ -388,14 +441,14 @@
         store.wait()
 
 
-def finish(hot, spectra, turned):
+def finish(hot, spectra, turned, per):
     chunks, traces_n, width = spectra.shape
     bins = chunks * width
     f32 = jnp.float32
     anywhere = pl.BlockSpec(memory_space=pl.ANY)
     dma = pltpu.SemaphoreType.DMA
     return pl.pallas_call(
-        finish_kernel,
+        functools.partial(finish_kernel, per),
         in_specs=[anywhere] * 3,
         out_specs=[anywhere] * 4,
         out_shape=[
@@ -422,7 +475,7 @@
     spectra, turned, hot = sweep(
         traces[0, 0], src, rcv, off, receiver_init, offset_init, nj, ny, nz
     )
-    return finish(hot, spectra, turned.reshape(-1, ROWS))
+    return finish(hot, spectra, turned.reshape(-1, ROWS), turned.shape[2])
 
 
 def solution(mesh):

time: 50.9 us -> 50.6 us (level)
    pallas_call x1, Pallas kernels: 46.8 us -> 46.2 us  [sweep(): pl.pallas_call(functools.partial(sweep_kernel, nj, ny, nz, groups), in_sp...]
where the time goes in v5:
time: 50.6 us; the launch traced here: 50.5 us
  Pallas kernels  49.8 us (98%)
  between operations  0.64 us (1%)
    pallas_call x1, Pallas kernels, sweep(): pl.pallas_call(functools.partial(sweep_kernel, nj, ny, nz, groups), in_sp...  46.2 us
    pallas_call x1, Pallas kernels, finish(): pl.pallas_call(functools.partial(finish_kernel, per), in_specs=[anywhere]...  3.67 us

profile of v5, /device:TPU:1, one launch (start us, length us, event | category | flops | bytes accessed | tf_op | source)
XLA Modules:
  0.0 50.5 jit_solution(3110567597397059271)
XLA Ops:
  0.6 46.2 %shard_map.102 = (f32[4,256,256]{2,1,0:T(8,128)}, f32[2,16,32,128]{3,2,1,0:T(8,128)}, bf16[256,128]{1,0:T(8,128)(2,1)}) custom-call(bf16[256,2048]{1,0:T(8,128)(2,1)} %bitcast.5, bf16[4,2048,512]{2,1,0:T(8,128)(2,1)} %constant.2.clone.tables_hbm, s32[1,256]{1,0:T(1,128)} %bitcast.7, s32[1,256]{1,0:T(1,128)} %bitcast.8, s32[1,256]{1,0:T(1,128)} %bitcast.9, ...), custom_call_target="tpu_custom_call" | custom-call | tf_op jit(solution)/shard_map/pallas_call | solution.py:348
  46.8 3.7 %shard_map.103 = (f32[32,1024]{1,0:T(8,128)}, f32[32,1024]{1,0:T(8,128)}, f32[64,1024]{1,0:T(8,128)}, f32[1,1,256,1024]{3,2,1,0:T(8,128)}) custom-call(bf16[256,128]{1,0:T(8,128)(2,1)} %get-tuple-element.7.hot_hbm, f32[4,256,256]{2,1,0:T(8,128)} %get-tuple-element.8.spectra_hbm, f32[1024,128]{1,0:T(8,128)} %bitcast.6), custom_call_target="tpu_custom_call" | custom-call | tf_op jit(solution)/shard_map/pallas_call | solution.py:450

commit v6 on v4

--- a/solution.py
+++ b/solution.py
@@ -73,8 +73,8 @@
     nj, ny, nz, groups,
     traces_hbm, tables_hbm, src_hbm, rcv_hbm, off_hbm, rinit_hbm, oinit_hbm,
     spectra_hbm, terms_hbm, hot_hbm,
-    traces_buf, tables_buf, ids_buf, init_buf, x_buf, hot_buf, sums_buf,
-    gy_buf, gz_buf, gr_buf, a_buf, flat_buf, p_buf, b1_buf, b2_buf, c_buf, d_out,
+    traces_buf, tables_buf, ids_buf, init_buf, shift_buf, x_buf, hot_buf, sums_buf,
+    gs_buf, gy_buf, gz_buf, gr_buf, a_buf, flat_buf, p_buf, b1_buf, b2_buf, t_buf, c_buf, d_out,
     load_sem, table_sem, store_sem, send_sem, recv_sem,
 ):
     i = lax.axis_index("src")
@@ -89,14 +89,13 @@
     each = nj // groups
     first = j // each
 
-    mine = ids_buf.at[j]
     loads = [
-        pltpu.make_async_copy(src_hbm, mine.at[0], load_sem.at[0]),
-        pltpu.make_async_copy(rcv_hbm, mine.at[1], load_sem.at[1]),
-        pltpu.make_async_copy(off_hbm, mine.at[2], load_sem.at[2]),
+        pltpu.make_async_copy(src_hbm, ids_buf.at[0], load_sem.at[0]),
+        pltpu.make_async_copy(rcv_hbm, ids_buf.at[1], load_sem.at[1]),
+        pltpu.make_async_copy(off_hbm, ids_buf.at[2], load_sem.at[2]),
         pltpu.make_async_copy(traces_hbm, traces_buf, load_sem.at[3]),
-        pltpu.make_async_copy(rinit_hbm, init_buf.at[pl.ds(0, NRCV)], load_sem.at[4]),
-        pltpu.make_async_copy(oinit_hbm, init_buf.at[pl.ds(NRCV, NOFF)], load_sem.at[5]),
+        pltpu.make_async_copy(rinit_hbm, init_buf.at[pl.ds(NSRC, NRCV)], load_sem.at[4]),
+        pltpu.make_async_copy(oinit_hbm, init_buf.at[pl.ds(NSRC + NRCV, NOFF)], load_sem.at[5]),
     ]
     order = [h * groups + lax.rem(first + k, groups) for h in range(HALVES) for k in range(groups)]
     tables = [
@@ -140,23 +139,29 @@
 
     for copy in loads[:3]:
         copy.wait()
-    hot = hot_rows(ids_buf[j, 0], ids_buf[j, 1], ids_buf[j, 2])
+    hot = hot_rows(ids_buf[0], ids_buf[1], ids_buf[2])
     hot_buf[...] = hot.T.astype(jnp.bfloat16)
     hot = hot.astype(jnp.bfloat16)
     gram = lax.dot_general(hot, hot, OVER_LANES, preferred_element_type=jnp.float32)
+    gs_buf[j] = gram[:NSRC]
     gy_buf[y] = gram[NSRC : NSRC + NRCV]
     row = lax.broadcasted_iota(jnp.int32, (ROWS, ROWS), 0)
     lane = lax.broadcasted_iota(jnp.int32, (ROWS, ROWS), 1)
     from_rcv = (lane >= NSRC) & (lane < NSRC + NRCV) & (row < NSRC)
     from_off = (lane >= NSRC + NRCV) & (row < NSRC + NRCV)
-    before = jnp.where(from_rcv | from_off, gram, 0.0).astype(jnp.bfloat16)[:, NSRC:]
+    before = jnp.where(from_rcv | from_off, gram, 0.0).astype(jnp.bfloat16)
     pl.semaphore_wait(barrier, nj + ny + nz - 3)
-    send(nj, over_j, j, lambda p: ids_buf.at[j], ids_buf, 0)
+    send(nj, over_j, j, lambda p: gs_buf.at[j], gs_buf, 0)
     stores = [pltpu.make_async_copy(hot_buf, hot_hbm, load_sem.at[0])]
     stores[0].start()
 
-    for copy in loads[3:]:
+    for copy in loads[4:]:
         copy.wait()
+    init_buf[:NSRC] = jnp.zeros((NSRC, init_buf.shape[1]), jnp.float32)
+    shift_buf[...] = dot(
+        jnp.concatenate([before, before], axis=1), jnp.concatenate(split(init_buf[...]), axis=0)
+    )
+    loads[3].wait()
     for n, c in enumerate(order):
         h, k = n // groups, n % groups
         g = c - h * groups
@@ -168,12 +173,9 @@
         store = pltpu.make_async_copy(x_buf.at[c], spectra_hbm.at[c], store_sem.at[n])
         store.start()
         stores.append(store)
-        init = init_buf[:, pl.ds(pl.multiple_of(c * width, width), width)]
         spec_high, spec_low = split(spectra)
-        init_high, init_low = split(init)
-        sums = (dot(hot, spec_high) - dot(before, init_high)) + (
-            dot(hot, spec_low) - dot(before, init_low)
-        )
+        span = pl.ds(pl.multiple_of(c * width, width), width)
+        sums = dot(hot, spec_high) + dot(hot, spec_low) - shift_buf[:, span]
         turned = sums.T
         for q in range(each):
             sums_buf[h, g * each + q] = turned[q * per : (q + 1) * per]
@@ -185,15 +187,8 @@
     for h in range(HALVES):
         a_buf[h, j] = sums_buf[h, j]
 
-    all_of(nj, over_j, ids_buf, 0).wait_recv()
-    by_src = []
-    for q in range(nj):
-        peer_hot = hot_rows(ids_buf[q, 0], ids_buf[q, 1], ids_buf[q, 2]).astype(jnp.bfloat16)
-        by_src.append(
-            lax.dot_general(
-                peer_hot[:NSRC], peer_hot, OVER_LANES, preferred_element_type=jnp.float32
-            )
-        )
+    all_of(nj, over_j, gs_buf, 0).wait_recv()
+    by_src = [gs_buf[q] for q in range(nj)]
     src_count = add(by_src)
     n_src = jnp.sum(src_count, axis=0, keepdims=True) + 1.0
     off_high, off_low = split(src_count)
@@ -232,8 +227,10 @@
         all_of(nz, over_z, b2_buf.at[h], 6 + 5 * h).wait_recv()
         reduced = add([b2_buf[h, q] for q in range(nz)])
         rcv_terms = reduced[:, : tiles * ROWS] / n_rcv
-        high, low = split(rcv_terms)
-        both = dot(high, by_rcv) + dot(low, by_rcv)
+        for k, part in enumerate(split(rcv_terms)):
+            t_buf[h, k * few : (k + 1) * few, :] = part.astype(jnp.float32)
+        both = dot(t_buf[h].astype(jnp.bfloat16), by_rcv)
+        both = both[:few] + both[few:]
         later = reduced[:, tiles * ROWS :] - both[:, :ROWS] - both[:, ROWS:]
         c_buf[h, y] = jnp.concatenate([rcv_terms, later / n_off], axis=1)
         send(ny, over_y, y, lambda p: c_buf.at[h, y], c_buf.at[h], 7 + 5 * h)
@@ -258,19 +255,31 @@
     src_low = source_step(0)
     src_high = source_step(1)
     all_of(nz, over_z, gz_buf, 2).wait_recv()
-    gr_buf[j] = jnp.sum(gz_buf[...], axis=0)
+    count = jnp.sum(gz_buf[...], axis=0)
+    half = NRCV // 2
+    wide = lax.broadcasted_iota(jnp.int32, (half, ROWS), 1) >= NSRC + NRCV
+    gr_buf[j] = jnp.where(wide, count[:half], pltpu.roll(count[half:], ROWS // 2, 1))
     send(nj, over_j, j, lambda p: gr_buf.at[j], gr_buf, 3)
     reduce_step(0)
     reduce_step(1)
 
     all_of(nj, over_j, gr_buf, 3).wait_recv()
-    by_rcv = gr_buf[...]
-    columns = [jnp.sum(by_rcv[q], axis=0, keepdims=True) for q in range(nj)]
-    n_off = add(columns) + 1.0
-    columns = [jnp.broadcast_to(c, (8, ROWS)) for c in columns]
-    n_rcv = [pick(columns[4 * t : 4 * t + 4], lane[:8])[:1] for t in range(tiles)]
-    n_rcv = jnp.concatenate(n_rcv, axis=1) + 1.0
-    by_rcv = jnp.concatenate(split(by_rcv.reshape(nj * NRCV, ROWS)), axis=1)
+    by_rcv = []
+    for q in range(nj):
+        packed = gr_buf[q]
+        by_rcv.append(jnp.where(wide, packed, 0.0))
+        by_rcv.append(jnp.where(wide, pltpu.roll(packed, ROWS // 2, 1), 0.0))
+    by_rcv = jnp.concatenate(by_rcv, axis=0)
+    n_off = jnp.sum(by_rcv, axis=0, keepdims=True) + 1.0
+    by_rcv = split(by_rcv)
+    ones = jnp.ones((16, ROWS), jnp.bfloat16)
+    n_rcv = add(
+        [
+            lax.dot_general(ones, part, OVER_LANES, preferred_element_type=jnp.float32)
+            for part in by_rcv
+        ]
+    )[:1] + 1.0
+    by_rcv = jnp.concatenate(by_rcv, axis=1)
 
     term_step(0)
     term_step(1)
@@ -278,7 +287,7 @@
     back_step(1, src_high)
 
     for phase, (n, over, buf) in enumerate(
-        [(nj, over_j, ids_buf), (ny, over_y, gy_buf), (nz, over_z, gz_buf), (nj, over_j, gr_buf)]
+        [(nj, over_j, gs_buf), (ny, over_y, gy_buf), (nz, over_z, gz_buf), (nj, over_j, gr_buf)]
     ):
         all_of(n, over, buf, phase).wait_send()
     for h in range(HALVES):
@@ -321,19 +330,22 @@
         scratch_shapes=[
             pltpu.VMEM((traces_n, samples), b16),
             pltpu.VMEM((chunks, samples, 2 * width), b16),
-            pltpu.VMEM((nj, 3, 1, traces_n), jnp.int32),
-            pltpu.VMEM((NRCV + NOFF, bins), f32),
+            pltpu.VMEM((3, 1, traces_n), jnp.int32),
+            pltpu.VMEM((ROWS, bins), f32),
+            pltpu.VMEM((ROWS, bins), f32),
             pltpu.VMEM((chunks, traces_n, width), f32),
             pltpu.VMEM((traces_n, ROWS), b16),
             pltpu.VMEM((HALVES, nj, per, ROWS), f32),
+            pltpu.VMEM((nj, NSRC, ROWS), f32),
             pltpu.VMEM((ny, NRCV, ROWS), f32),
             pltpu.VMEM((nz, NRCV, ROWS), f32),
-            pltpu.VMEM((nj, NRCV, ROWS), f32),
+            pltpu.VMEM((nj, NRCV // 2, ROWS), f32),
             pltpu.VMEM((HALVES, nj, per, ROWS), f32),
             pltpu.VMEM((HALVES, per, wide), f32),
             pltpu.VMEM((HALVES, ny, few, wide), f32),
             pltpu.VMEM((HALVES, ny, few, wide), f32),
             pltpu.VMEM((HALVES, nz, few, wide), f32),
+            pltpu.VMEM((HALVES, 2 * few, nj * NRCV), f32),
             pltpu.VMEM((HALVES, ny, few, wide), f32),
             pltpu.VMEM((HALVES, nj, per, ROWS), f32),
             dma((6,)), dma((chunks,)), dma((chunks,)), dma((phases,)), dma((phases,)),
@@ -361,16 +373,15 @@
         for copy in parts[c]:
             copy.start()
     load.wait()
-    hot = hot_buf[...]
+    hot = jnp.concatenate([hot_buf[...]] * 2, axis=1)
     stores = []
     for c in range(chunks):
         for copy in parts[c]:
             copy.wait()
         span = slice(c * width, (c + 1) * width)
         turned = turned_buf[span]
-        high, low = split(turned)
-        spread = lax.dot_general(hot, high, OVER_LANES, preferred_element_type=jnp.float32)
-        spread += lax.dot_general(hot, low, OVER_LANES, preferred_element_type=jnp.float32)
+        both = jnp.concatenate(split(turned), axis=1)
+        spread = lax.dot_general(hot, both, OVER_LANES, preferred_element_type=jnp.float32)
         x_buf[c] = x_buf[c] - spread
         store = pltpu.make_async_copy(
             x_buf.at[c], residual_out.at[0, 0, :, pl.ds(c * width, width)], store_sem.at[c]

time: 50.9 us -> 52 us (1.022)
  Pallas kernels: 50.1 us -> 51 us
    pallas_call x1, Pallas kernels: 46.8 us -> 47.8 us  [sweep(): pl.pallas_call(functools.partial(sweep_kernel, nj, ny, nz, groups), in_sp...]
where the time goes in v6:
time: 52 us; the launch traced here: 51.7 us
  Pallas kernels  51 us (98%)
  between operations  0.64 us (1%)
    pallas_call x1, Pallas kernels, sweep(): pl.pallas_call(functools.partial(sweep_kernel, nj, ny, nz, groups), in_sp...  47.8 us
    pallas_call x1, Pallas kernels, finish(): pl.pallas_call(finish_kernel, in_specs=[anywhere] * 3, out_specs=[anywher...  3.2 us

profile of v6, /device:TPU:1, one launch (start us, length us, event | category | flops | bytes accessed | tf_op | source)
XLA Modules:
  0.0 51.7 jit_solution(9976695812605119439)
XLA Ops:
  0.6 47.8 %shard_map.102 = (f32[4,256,256]{2,1,0:T(8,128)}, f32[2,16,32,128]{3,2,1,0:T(8,128)}, bf16[256,128]{1,0:T(8,128)(2,1)}) custom-call(bf16[256,2048]{1,0:T(8,128)(2,1)} %bitcast.5, bf16[4,2048,512]{2,1,0:T(8,128)(2,1)} %constant.2.clone.tables_hbm, s32[1,256]{1,0:T(1,128)} %bitcast.7, s32[1,256]{1,0:T(1,128)} %bitcast.8, s32[1,256]{1,0:T(1,128)} %bitcast.9, ...), custom_call_target="tpu_custom_call" | custom-call | tf_op jit(solution)/shard_map/pallas_call | solution.py:321
  48.5 3.2 %shard_map.103 = (f32[32,1024]{1,0:T(8,128)}, f32[32,1024]{1,0:T(8,128)}, f32[64,1024]{1,0:T(8,128)}, f32[1,1,256,1024]{3,2,1,0:T(8,128)}) custom-call(bf16[256,128]{1,0:T(8,128)(2,1)} %get-tuple-element.7.hot_hbm, f32[4,256,256]{2,1,0:T(8,128)} %get-tuple-element.8.spectra_hbm, f32[1024,128]{1,0:T(8,128)} %bitcast.6), custom_call_target="tpu_custom_call" | custom-call | tf_op jit(solution)/shard_map/pallas_call | solution.py:408

commit v7 on v6

--- a/solution.py
+++ b/solution.py
@@ -74,7 +74,7 @@
     traces_hbm, tables_hbm, src_hbm, rcv_hbm, off_hbm, rinit_hbm, oinit_hbm,
     spectra_hbm, terms_hbm, hot_hbm,
     traces_buf, tables_buf, ids_buf, init_buf, shift_buf, x_buf, hot_buf, sums_buf,
-    gs_buf, gy_buf, gz_buf, gr_buf, a_buf, flat_buf, p_buf, b1_buf, b2_buf, t_buf, c_buf, d_out,
+    gs_buf, gy_buf, gz_buf, gr_buf, a_buf, flat_buf, p_buf, b1_buf, b2_buf, t_buf, c_buf, d_out, d_buf, f_out,
     load_sem, table_sem, store_sem, send_sem, recv_sem,
 ):
     i = lax.axis_index("src")
@@ -85,7 +85,12 @@
     width = x_buf.shape[2]
     per = a_buf.shape[2]
     few = per // ny
+    quarter = per // 4
     tiles = nj * NRCV // ROWS
+    chips = nj // 2
+    chip = j // 2
+    core = lax.rem(j, 2)
+    partner = (i, j + 1 - 2 * core)
     each = nj // groups
     first = j // each
 
@@ -116,6 +121,10 @@
     def over_z(d):
         peer = lax.rem(z + d, nz)
         return peer, (y * nz + peer, j)
+
+    def over_chips(d):
+        peer = lax.rem(chip + d, chips)
+        return peer, (i, 2 * peer + core)
 
     def copy_to(device, source, target, phase):
         return pltpu.make_async_remote_copy(
@@ -242,16 +251,39 @@
         off_tile = flat_buf[h, :, tiles * ROWS :]
         for t in range(tiles):
             tile = flat_buf[h, :, t * ROWS : (t + 1) * ROWS]
-            for q in range(4):
-                turned = tile if q == 1 else pltpu.roll(tile, (32 - 32 * q) % ROWS, 1)
-                d_out[h, 4 * t + q] = jnp.where(
-                    lane < NSRC, src_terms, jnp.where(lane < NSRC + NRCV, turned, off_tile)
+            for k in range(2):
+                zero = pltpu.roll(tile, (32 - 64 * k) % ROWS, 1)
+                one = pltpu.roll(tile, (-64 * k) % ROWS, 1) if k else tile
+                same = jnp.where(is_zero, zero, one)
+                other = jnp.where(is_zero, one, zero)
+                d_out[h, 2 * t + k, :per, :] = jnp.where(
+                    lane < NSRC, src_terms, jnp.where(lane < NSRC + NRCV, same, off_tile)
                 )
-        send(nj, over_j, j, lambda p: d_out.at[h, p], terms_hbm.at[h], 8 + 5 * h)
-        own = pltpu.make_async_copy(d_out.at[h, j], terms_hbm.at[h, j], load_sem.at[1 + h])
+                parts = [other[q * quarter : (q + 1) * quarter] for q in range(4)]
+                d_out[h, 2 * t + k, per:, :] = pick(parts, lane[:quarter])
+        send(chips, over_chips, chip, lambda p: d_out.at[h, p], d_buf.at[h], 8 + 5 * h)
+        d_buf[h, chip] = d_out[h, chip]
+
+    def pair_copy(h, place):
+        return copy_to(partner, f_out.at[h], terms_hbm.at[h, place], 4 + 5 * HALVES + h)
+
+    def pair_step(h):
+        all_of(chips, over_chips, d_buf.at[h], 8 + 5 * h).wait_recv()
+        own = pltpu.make_async_copy(
+            d_buf.at[h, :, pl.ds(0, per)], terms_hbm.at[h, core], load_sem.at[1 + h]
+        )
         own.start()
         stores.append(own)
-
+        inside = (lane[:quarter] >= NSRC) & (lane[:quarter] < NSRC + NRCV)
+        for p in range(chips):
+            packed = d_buf[h, p, per:, :]
+            for q in range(4):
+                rows = slice(q * quarter, (q + 1) * quarter)
+                other = packed if q == 1 else pltpu.roll(packed, (32 - 32 * q) % ROWS, 1)
+                f_out[h, p, rows, :] = jnp.where(inside, other, d_buf[h, p, rows, :])
+        pair_copy(h, core).start()
+
+    is_zero = jnp.zeros((per, ROWS), jnp.int32) + core == 0
     src_low = source_step(0)
     src_high = source_step(1)
     all_of(nz, over_z, gz_buf, 2).wait_recv()
@@ -285,6 +317,8 @@
     term_step(1)
     back_step(0, src_low)
     back_step(1, src_high)
+    pair_step(0)
+    pair_step(1)
 
     for phase, (n, over, buf) in enumerate(
         [(nj, over_j, gs_buf), (ny, over_y, gy_buf), (nz, over_z, gz_buf), (nj, over_j, gr_buf)]
@@ -294,14 +328,15 @@
         for phase, (n, over, buf) in enumerate(
             [
                 (nj, over_j, a_buf), (ny, over_y, b1_buf), (nz, over_z, b2_buf),
-                (ny, over_y, c_buf), (nj, over_j, d_out),
+                (ny, over_y, c_buf), (chips, over_chips, d_buf),
             ]
         ):
             all_of(n, over, buf.at[h], 4 + 5 * h + phase).wait_send()
     for store in stores:
         store.wait()
     for h in range(HALVES):
-        all_of(nj, over_j, terms_hbm.at[h], 8 + 5 * h).wait_recv()
+        pair_copy(h, core).wait_send()
+        pair_copy(h, 1 - core).wait_recv()
 
 
 def sweep(traces, src, rcv, off, receiver_init, offset_init, nj, ny, nz):
@@ -317,14 +352,14 @@
     tables = jnp.asarray(dft_tables(samples, bins, chunks))
     anywhere = pl.BlockSpec(memory_space=pl.ANY)
     dma = pltpu.SemaphoreType.DMA
-    phases = 4 + 5 * HALVES
+    phases = 4 + 6 * HALVES
     return pl.pallas_call(
         functools.partial(sweep_kernel, nj, ny, nz, groups),
         in_specs=[anywhere] * 7,
         out_specs=[anywhere] * 3,
         out_shape=[
             jax.ShapeDtypeStruct((chunks, traces_n, width), f32),
-            jax.ShapeDtypeStruct((HALVES, nj, per, ROWS), f32),
+            jax.ShapeDtypeStruct((HALVES, 2, nj // 2, per, ROWS), f32),
             jax.ShapeDtypeStruct((traces_n, ROWS), b16),
         ],
         scratch_shapes=[
@@ -347,7 +382,9 @@
             pltpu.VMEM((HALVES, nz, few, wide), f32),
             pltpu.VMEM((HALVES, 2 * few, nj * NRCV), f32),
             pltpu.VMEM((HALVES, ny, few, wide), f32),
-            pltpu.VMEM((HALVES, nj, per, ROWS), f32),
+            pltpu.VMEM((HALVES, nj // 2, per + per // 4, ROWS), f32),
+            pltpu.VMEM((HALVES, nj // 2, per + per // 4, ROWS), f32),
+            pltpu.VMEM((HALVES, nj // 2, per, ROWS), f32),
             dma((6,)), dma((chunks,)), dma((chunks,)), dma((phases,)), dma((phases,)),
         ],
         compiler_params=pltpu.CompilerParams(
@@ -364,10 +401,12 @@
     load = pltpu.make_async_copy(hot_hbm, hot_buf, load_sem.at[0])
     load.start()
     parts = []
+    _, cores, taken, _, _ = turned_buf.shape
+    groups = chunks // HALVES
     for c in range(chunks):
-        rows = pl.ds(c * width, width)
+        source = turned_hbm.at[c // groups, :, pl.ds(c % groups * taken, taken)]
         parts.append((
-            pltpu.make_async_copy(turned_hbm.at[rows], turned_buf.at[rows], turned_sem.at[c]),
+            pltpu.make_async_copy(source, turned_buf.at[c], turned_sem.at[c]),
             pltpu.make_async_copy(spectra_hbm.at[c], x_buf.at[c], x_sem.at[c]),
         ))
         for copy in parts[c]:
@@ -379,7 +418,9 @@
         for copy in parts[c]:
             copy.wait()
         span = slice(c * width, (c + 1) * width)
-        turned = turned_buf[span]
+        turned = jnp.concatenate(
+            [turned_buf[c, core, p] for p in range(taken) for core in range(cores)], axis=0
+        )
         both = jnp.concatenate(split(turned), axis=1)
         spread = lax.dot_general(hot, both, OVER_LANES, preferred_element_type=jnp.float32)
         x_buf[c] = x_buf[c] - spread
@@ -402,6 +443,8 @@
 def finish(hot, spectra, turned):
     chunks, traces_n, width = spectra.shape
     bins = chunks * width
+    halves, cores, chips, per, rows = turned.shape
+    taken = chips * halves // chunks
     f32 = jnp.float32
     anywhere = pl.BlockSpec(memory_space=pl.ANY)
     dma = pltpu.SemaphoreType.DMA
@@ -418,7 +461,7 @@
         scratch_shapes=[
             pltpu.VMEM(hot.shape, hot.dtype),
             pltpu.VMEM(spectra.shape, f32),
-            pltpu.VMEM(turned.shape, f32),
+            pltpu.VMEM((chunks, cores, taken, per, rows), f32),
             pltpu.VMEM((ROWS, bins), f32),
             dma((1,)), dma((chunks,)), dma((chunks,)), dma((chunks,)), dma((3,)),
         ],
@@ -433,7 +476,7 @@
     spectra, turned, hot = sweep(
         traces[0, 0], src, rcv, off, receiver_init, offset_init, nj, ny, nz
     )
-    return finish(hot, spectra, turned.reshape(-1, ROWS))
+    return finish(hot, spectra, turned)
 
 
 def solution(mesh):

time: 52 us -> 52.2 us (level)
  no operation moved by 1% of the time
where the time goes in v7:
time: 52.2 us; the launch traced here: 52 us
  Pallas kernels  51.4 us (98%)
  between operations  0.64 us (1%)
    pallas_call x1, Pallas kernels, sweep(): pl.pallas_call(functools.partial(sweep_kernel, nj, ny, nz, groups), in_sp...  48.2 us
    pallas_call x1, Pallas kernels, finish(): pl.pallas_call(finish_kernel, in_specs=[anywhere] * 3, out_specs=[anywher...  3.2 us

profile of v7, /device:TPU:1, one launch (start us, length us, event | category | flops | bytes accessed | tf_op | source)
XLA Modules:
  0.0 52.0 jit_solution(480537200111350479)
XLA Ops:
  0.6 48.2 %shard_map.102 = (f32[4,256,256]{2,1,0:T(8,128)}, f32[2,2,8,32,128]{4,3,2,1,0:T(8,128)}, bf16[256,128]{1,0:T(8,128)(2,1)}) custom-call(bf16[256,2048]{1,0:T(8,128)(2,1)} %bitcast.4, bf16[4,2048,512]{2,1,0:T(8,128)(2,1)} %constant.2.clone.tables_hbm, s32[1,256]{1,0:T(1,128)} %bitcast.5, s32[1,256]{1,0:T(1,128)} %bitcast.6, s32[1,256]{1,0:T(1,128)} %bitcast.7, ...), custom_call_target="tpu_custom_call" | custom-call | tf_op jit(solution)/shard_map/pallas_call | solution.py:356
  48.8 3.2 %shard_map.103 = (f32[32,1024]{1,0:T(8,128)}, f32[32,1024]{1,0:T(8,128)}, f32[64,1024]{1,0:T(8,128)}, f32[1,1,256,1024]{3,2,1,0:T(8,128)}) custom-call(bf16[256,128]{1,0:T(8,128)(2,1)} %get-tuple-element.7.hot_hbm, f32[4,256,256]{2,1,0:T(8,128)} %get-tuple-element.8.spectra_hbm, f32[2,2,8,32,128]{4,3,2,1,0:T(8,128)} %get-tuple-element.9.turned_hbm), custom_call_target="tpu_custom_call" | custom-call | tf_op jit(solution)/shard_map/pallas_call | solution.py:451

commit v8 on v5

--- a/solution.py
+++ b/solution.py
@@ -73,8 +73,8 @@
     nj, ny, nz, groups,
     traces_hbm, tables_hbm, src_hbm, rcv_hbm, off_hbm, rinit_hbm, oinit_hbm,
     spectra_hbm, terms_hbm, hot_hbm,
-    traces_buf, tables_buf, ids_buf, init_buf, x_buf, hot_buf, sums_buf,
-    gy_buf, gz_buf, gr_buf, a_buf, s_buf, flat_buf, p_buf, b1_buf, b2_buf, c_buf, d_out,
+    traces_buf, tables_buf, ids_buf, init_buf, shift_buf, x_buf, hot_buf, sums_buf,
+    gy_buf, gz_buf, gr_buf, a_buf, s_buf, flat_buf, p_buf, b1_buf, b2_buf, t_buf, c_buf, d_out,
     load_sem, table_sem, store_sem, send_sem, recv_sem,
 ):
     i = lax.axis_index("src")
@@ -96,8 +96,8 @@
         pltpu.make_async_copy(rcv_hbm, mine.at[1], load_sem.at[1]),
         pltpu.make_async_copy(off_hbm, mine.at[2], load_sem.at[2]),
         pltpu.make_async_copy(traces_hbm, traces_buf, load_sem.at[3]),
-        pltpu.make_async_copy(rinit_hbm, init_buf.at[pl.ds(0, NRCV)], load_sem.at[4]),
-        pltpu.make_async_copy(oinit_hbm, init_buf.at[pl.ds(NRCV, NOFF)], load_sem.at[5]),
+        pltpu.make_async_copy(rinit_hbm, init_buf.at[pl.ds(NSRC, NRCV)], load_sem.at[4]),
+        pltpu.make_async_copy(oinit_hbm, init_buf.at[pl.ds(NSRC + NRCV, NOFF)], load_sem.at[5]),
     ]
     order = [h * groups + lax.rem(first + k, groups) for h in range(HALVES) for k in range(groups)]
     tables = [
@@ -150,31 +150,37 @@
     lane = lax.broadcasted_iota(jnp.int32, (ROWS, ROWS), 1)
     from_rcv = (lane >= NSRC) & (lane < NSRC + NRCV) & (row < NSRC)
     from_off = (lane >= NSRC + NRCV) & (row < NSRC + NRCV)
-    before = jnp.where(from_rcv | from_off, gram, 0.0).astype(jnp.bfloat16)[:, NSRC:]
+    before = jnp.where(from_rcv | from_off, gram, 0.0).astype(jnp.bfloat16)
     pl.semaphore_wait(barrier, nj + ny + nz - 3)
     send(nj, over_j, j, lambda p: ids_buf.at[j], ids_buf, 0)
     stores = [pltpu.make_async_copy(hot_buf, hot_hbm, load_sem.at[0])]
     stores[0].start()
 
-    for copy in loads[3:]:
+    for copy in loads[4:]:
         copy.wait()
+    init_buf[:NSRC] = jnp.zeros((NSRC, init_buf.shape[1]), jnp.float32)
+    shift_buf[...] = dot(
+        jnp.concatenate([before, before], axis=1), jnp.concatenate(split(init_buf[...]), axis=0)
+    )
+    loads[3].wait()
+    tables[0].wait()
+    ahead = dot(traces_buf[...], tables_buf[order[0]])
     for n, c in enumerate(order):
         h, k = n // groups, n % groups
         g = c - h * groups
-        tables[n].wait()
-        both = dot(traces_buf[...], tables_buf[c])
+        both = ahead
+        if n + 1 < len(order):
+            tables[n + 1].wait()
+            ahead = dot(traces_buf[...], tables_buf[order[n + 1]])
         real, imag = both[:, :width], both[:, width:]
         spectra = 0.5 * jnp.log((real * real + imag * imag) * (1.0 / samples) + 0.25)
         x_buf[c] = spectra
         store = pltpu.make_async_copy(x_buf.at[c], spectra_hbm.at[c], store_sem.at[n])
         store.start()
         stores.append(store)
-        init = init_buf[:, pl.ds(pl.multiple_of(c * width, width), width)]
         spec_high, spec_low = split(spectra)
-        init_high, init_low = split(init)
-        sums = (dot(hot, spec_high) - dot(before, init_high)) + (
-            dot(hot, spec_low) - dot(before, init_low)
-        )
+        span = pl.ds(pl.multiple_of(c * width, width), width)
+        sums = dot(hot, spec_high) + dot(hot, spec_low) - shift_buf[:, span]
         turned = sums.T
         for q in range(each):
             sums_buf[h, g * each + q] = turned[q * per : (q + 1) * per]
@@ -234,8 +240,10 @@
         all_of(nz, over_z, b2_buf.at[h], 6 + 5 * h).wait_recv()
         reduced = add([b2_buf[h, q] for q in range(nz)])
         rcv_terms = reduced[:, : tiles * ROWS] / n_rcv
-        high, low = split(rcv_terms)
-        both = dot(high, by_rcv) + dot(low, by_rcv)
+        for k, part in enumerate(split(rcv_terms)):
+            t_buf[h, k * few : (k + 1) * few, :] = part.astype(jnp.float32)
+        both = dot(t_buf[h].astype(jnp.bfloat16), by_rcv)
+        both = both[:few] + both[few:]
         later = reduced[:, tiles * ROWS :] - both[:, :ROWS] - both[:, ROWS:]
         c_buf[h, y] = jnp.concatenate([rcv_terms, later / n_off], axis=1)
         send(ny, over_y, y, lambda p: c_buf.at[h, y], c_buf.at[h], 7 + 5 * h)
@@ -358,7 +366,8 @@
             pltpu.VMEM((traces_n, samples), b16),
             pltpu.VMEM((chunks, samples, 2 * width), b16),
             pltpu.VMEM((nj, 3, 1, traces_n), jnp.int32),
-            pltpu.VMEM((NRCV + NOFF, bins), f32),
+            pltpu.VMEM((ROWS, bins), f32),
+            pltpu.VMEM((ROWS, bins), f32),
             pltpu.VMEM((chunks, traces_n, width), f32),
             pltpu.VMEM((traces_n, ROWS), b16),
             pltpu.VMEM((HALVES, nj, per, ROWS), f32),
@@ -371,6 +380,7 @@
             pltpu.VMEM((HALVES, ny, few, wide), f32),
             pltpu.VMEM((HALVES, ny, few, wide), f32),
             pltpu.VMEM((HALVES, nz, few, wide), f32),
+            pltpu.VMEM((HALVES, 2 * few, nj * NRCV), f32),
             pltpu.VMEM((HALVES, ny, few, wide), f32),
             pltpu.VMEM((HALVES, nj, per // 4 * 3, ROWS), f32),
             dma((6,)), dma((chunks,)), dma((chunks,)), dma((phases,)), dma((phases,)),
@@ -414,16 +424,15 @@
         for copy in parts[c]:
             copy.start()
     load.wait()
-    hot = hot_buf[...]
+    hot = jnp.concatenate([hot_buf[...]] * 2, axis=1)
     stores = []
     for c in range(chunks):
         for copy in parts[c]:
             copy.wait()
         span = slice(c * width, (c + 1) * width)
         turned = unpack(turned_buf[span], per)
-        high, low = split(turned)
-        spread = lax.dot_general(hot, high, OVER_LANES, preferred_element_type=jnp.float32)
-        spread += lax.dot_general(hot, low, OVER_LANES, preferred_element_type=jnp.float32)
+        both = jnp.concatenate(split(turned), axis=1)
+        spread = lax.dot_general(hot, both, OVER_LANES, preferred_element_type=jnp.float32)
         x_buf[c] = x_buf[c] - spread
         store = pltpu.make_async_copy(
             x_buf.at[c], residual_out.at[0, 0, :, pl.ds(c * width, width)], store_sem.at[c]

time: 50.6 us -> 51 us (level)
    pallas_call x1, Pallas kernels: 46.2 us -> 46.8 us  [sweep(): pl.pallas_call(functools.partial(sweep_kernel, nj, ny, nz, groups), in_sp...]
where the time goes in v8:
time: 51 us; the launch traced here: 50.9 us
  Pallas kernels  50.2 us (98%)
  between operations  0.64 us (1%)
    pallas_call x1, Pallas kernels, sweep(): pl.pallas_call(functools.partial(sweep_kernel, nj, ny, nz, groups), in_sp...  46.8 us
    pallas_call x1, Pallas kernels, finish(): pl.pallas_call(functools.partial(finish_kernel, per), in_specs=[anywhere]...  3.46 us

profile of v8, /device:TPU:1, one launch (start us, length us, event | category | flops | bytes accessed | tf_op | source)
XLA Modules:
  0.0 50.9 jit_solution(6543166860358306308)
XLA Ops:
  0.6 46.8 %shard_map.102 = (f32[4,256,256]{2,1,0:T(8,128)}, f32[2,16,32,128]{3,2,1,0:T(8,128)}, bf16[256,128]{1,0:T(8,128)(2,1)}) custom-call(bf16[256,2048]{1,0:T(8,128)(2,1)} %bitcast.5, bf16[4,2048,512]{2,1,0:T(8,128)(2,1)} %constant.2.clone.tables_hbm, s32[1,256]{1,0:T(1,128)} %bitcast.7, s32[1,256]{1,0:T(1,128)} %bitcast.8, s32[1,256]{1,0:T(1,128)} %bitcast.9, ...), custom_call_target="tpu_custom_call" | custom-call | tf_op jit(solution)/shard_map/pallas_call | solution.py:356
  47.4 3.5 %shard_map.103 = (f32[32,1024]{1,0:T(8,128)}, f32[32,1024]{1,0:T(8,128)}, f32[64,1024]{1,0:T(8,128)}, f32[1,1,256,1024]{3,2,1,0:T(8,128)}) custom-call(bf16[256,128]{1,0:T(8,128)(2,1)} %get-tuple-element.7.hot_hbm, f32[4,256,256]{2,1,0:T(8,128)} %get-tuple-element.8.spectra_hbm, f32[1024,128]{1,0:T(8,128)} %bitcast.6), custom_call_target="tpu_custom_call" | custom-call | tf_op jit(solution)/shard_map/pallas_call | solution.py:459

commit v9 on v8

--- a/solution.py
+++ b/solution.py
@@ -248,14 +248,17 @@
         c_buf[h, y] = jnp.concatenate([rcv_terms, later / n_off], axis=1)
         send(ny, over_y, y, lambda p: c_buf.at[h, y], c_buf.at[h], 7 + 5 * h)
 
-    def source_out(h):
-        send(
-            nj, over_j, j, lambda p: s_buf.at[h],
-            terms_hbm.at[h, :, pl.ds(3 * quarter, quarter)], 4 + 5 * HALVES + h,
-        )
-        own = pltpu.make_async_copy(
-            s_buf.at[h], terms_hbm.at[h, j, pl.ds(3 * quarter, quarter)], load_sem.at[3 + h]
-        )
+    def source_part(place):
+        return terms_hbm.at[:, place, pl.ds(3 * quarter, quarter)]
+
+    def sources_sent():
+        part = source_part(pl.ds(0, nj - 1))
+        return copy_to(over_j(1)[1], part, part, 4 + 5 * HALVES)
+
+    def source_out():
+        for d in range(1, nj):
+            copy_to(over_j(d)[1], s_buf, source_part(j), 4 + 5 * HALVES).start()
+        own = pltpu.make_async_copy(s_buf, source_part(j), load_sem.at[3])
         own.start()
         stores.append(own)
 
@@ -290,8 +293,6 @@
     wide = lax.broadcasted_iota(jnp.int32, (half, ROWS), 1) >= NSRC + NRCV
     gr_buf[j] = jnp.where(wide, count[:half], pltpu.roll(count[half:], ROWS // 2, 1))
     send(nj, over_j, j, lambda p: gr_buf.at[j], gr_buf, 3)
-    for h in range(HALVES):
-        source_out(h)
     reduce_step(0)
     reduce_step(1)
 
@@ -315,6 +316,7 @@
 
     term_step(0)
     term_step(1)
+    source_out()
     back_step(0)
     back_step(1)
 
@@ -330,9 +332,8 @@
             ]
         ):
             all_of(n, over, buf.at[h], 4 + 5 * h + phase).wait_send()
-        sources = terms_hbm.at[h, :, pl.ds(3 * quarter, quarter)]
-        all_of(nj, over_j, sources, 4 + 5 * HALVES + h).wait_send()
-        all_of(nj, over_j, sources, 4 + 5 * HALVES + h).wait_recv()
+    sources_sent().wait_send()
+    sources_sent().wait_recv()
     for store in stores:
         store.wait()
     for h in range(HALVES):
@@ -352,7 +353,7 @@
     tables = jnp.asarray(dft_tables(samples, bins, chunks))
     anywhere = pl.BlockSpec(memory_space=pl.ANY)
     dma = pltpu.SemaphoreType.DMA
-    phases = 4 + 6 * HALVES
+    phases = 5 + 5 * HALVES
     return pl.pallas_call(
         functools.partial(sweep_kernel, nj, ny, nz, groups),
         in_specs=[anywhere] * 7,

time: 51 us -> 51 us (level)
  no operation moved by 1% of the time
where the time goes in v9:
time: 51 us; the launch traced here: 50.8 us
  Pallas kernels  50.2 us (98%)
  between operations  0.64 us (1%)
    pallas_call x1, Pallas kernels, sweep(): pl.pallas_call(functools.partial(sweep_kernel, nj, ny, nz, groups), in_sp...  46.7 us
    pallas_call x1, Pallas kernels, finish(): pl.pallas_call(functools.partial(finish_kernel, per), in_specs=[anywhere]...  3.47 us

profile of v9, /device:TPU:1, one launch (start us, length us, event | category | flops | bytes accessed | tf_op | source)
XLA Modules:
  0.0 50.8 jit_solution(16055151411393784738)
XLA Ops:
  0.6 46.7 %shard_map.102 = (f32[4,256,256]{2,1,0:T(8,128)}, f32[2,16,32,128]{3,2,1,0:T(8,128)}, bf16[256,128]{1,0:T(8,128)(2,1)}) custom-call(bf16[256,2048]{1,0:T(8,128)(2,1)} %bitcast.5, bf16[4,2048,512]{2,1,0:T(8,128)(2,1)} %constant.2.clone.tables_hbm, s32[1,256]{1,0:T(1,128)} %bitcast.7, s32[1,256]{1,0:T(1,128)} %bitcast.8, s32[1,256]{1,0:T(1,128)} %bitcast.9, ...), custom_call_target="tpu_custom_call" | custom-call | tf_op jit(solution)/shard_map/pallas_call | solution.py:357
  47.4 3.5 %shard_map.103 = (f32[32,1024]{1,0:T(8,128)}, f32[32,1024]{1,0:T(8,128)}, f32[64,1024]{1,0:T(8,128)}, f32[1,1,256,1024]{3,2,1,0:T(8,128)}) custom-call(bf16[256,128]{1,0:T(8,128)(2,1)} %get-tuple-element.7.hot_hbm, f32[4,256,256]{2,1,0:T(8,128)} %get-tuple-element.8.spectra_hbm, f32[1024,128]{1,0:T(8,128)} %bitcast.6), custom_call_target="tpu_custom_call" | custom-call | tf_op jit(solution)/shard_map/pallas_call | solution.py:460
